TPU v7x, 32 devices: a whole 2x2x4 slice. The times are simulated.
32 devices in a mesh: section: 2 (over core), ctx: 4 (over z), mp: 4 (over y, x).
Axes of the slice: x: 2, y: 2, z: 4, core: 2. Of those that a mesh axis runs over, the one named last changes fastest.
Arguments:
- hidden: bfloat16 [2, 512, 4672], P('section', 'ctx', 'mp'), may hold values from -120 to 120
- query: bfloat16 [2, 512, 2048], P('section', 'ctx', 'mp'), may hold values from -6 to 6
- keys: bfloat16 [2, 512, 2048], P('section', 'ctx', 'mp'), may hold values from -100 to 100
- values: bfloat16 [2, 512, 2048], P('section', 'ctx', 'mp'), may hold values from -12 to 12
- w_out: bfloat16 [2, 4672, 2048], P('section', 'ctx', 'mp'), may hold values from -0.125 to 0.125
Outputs:
- handed: bfloat16 [2, 512, 4672], P('section', 'ctx', 'mp')
- context: bfloat16 [2, 512, 2048], P('section', 'ctx', 'mp')
All inputs are finite; a program needn't handle non-finite values.
Results may differ from a plain program's by a relative error of at most 0.0075.
Values may be sent and summed in bfloat16 or wider, within the bound.
A program may use at most 128 MiB of HBM per device.

v0:
```python
import jax
import jax.numpy as jnp
from jax import lax
from jax.sharding import PartitionSpec as P

HEAD_DIM = 64


def from_behind(block, axis, distance):
    devices = range(lax.axis_size(axis))
    route = [((i - distance) % len(devices), i) for i in devices]
    return lax.ppermute(block, axis, route)


def head_scores(query_h, keys_h):
    return jnp.einsum("qd,kd->qk", query_h, keys_h, preferred_element_type=jnp.float32)


def body(hidden, query, keys, values, w_out):
    rows = hidden[0]
    query_rows = query[0]
    inner_dev = query_rows.shape[1]
    heads_dev = inner_dev // HEAD_DIM
    keys_local = keys[0]
    values_local = values[0]
    keys_all, values_all = (
        lax.all_gather(keys_local, "ctx", axis=0, tiled=True),
        lax.all_gather(values_local, "ctx", axis=0, tiled=True),
    )
    pieces = []
    for head in range(heads_dev):
        lower = head * HEAD_DIM
        upper = lower + HEAD_DIM
        scores = head_scores(query_rows[:, lower:upper], keys_all[:, lower:upper])
        peak = jnp.max(scores, axis=1, keepdims=True)
        expo = jnp.exp(scores - peak)
        total = jnp.sum(expo, axis=1, keepdims=True)
        summed = jnp.dot(
            expo.astype(jnp.bfloat16),
            values_all[:, lower:upper],
            preferred_element_type=jnp.float32,
        )
        pieces.append(summed / total)
    context = jnp.concatenate(pieces, axis=1).astype(jnp.bfloat16)
    out_local = w_out[0]
    context_all = lax.all_gather(context, "ctx", axis=0, tiled=True)
    projected = jnp.einsum(
        "ri,di->rd", context_all, out_local, preferred_element_type=jnp.float32
    ).astype(jnp.bfloat16)
    branch_terms = lax.all_to_all(projected, "ctx", split_axis=0, concat_axis=1, tiled=True).astype(
        jnp.float32
    )
    branch = lax.psum_scatter(
        branch_terms.astype(jnp.bfloat16), "mp", scatter_dimension=1, tiled=True
    ).astype(jnp.float32)
    result = (rows.astype(jnp.float32) + branch).astype(jnp.bfloat16)
    handed = from_behind(result, "section", 1)
    return (handed[None], context[None])


def solution(mesh):
    in_specs = (
        P("section", "ctx", "mp"),
        P("section", "ctx", "mp"),
        P("section", "ctx", "mp"),
        P("section", "ctx", "mp"),
        P("section", "ctx", "mp"),
    )
    out_specs = (P("section", "ctx", "mp"), P("section", "ctx", "mp"))
    return jax.shard_map(body, mesh=mesh, in_specs=in_specs, out_specs=out_specs, check_vma=False)
```

profile of v0, /device:TPU:1, one launch (start us, length us, event | category | flops | bytes accessed | tf_op | source)
XLA Modules:
  0.0 128.1 jit_solution(11860358959307707989)
XLA Ops:
  7.2 0.0 copy-start
  7.2 0.0 copy-start.1
  7.2 0.0 reduce-scatter.4.cloned.1.call-start
  7.2 15.6 %all-gather = bf16[1,512,512]{2,1,0:T(8,128)(2,1)S(1)} all-gather(bf16[1,128,512]{2,1,0:T(8,128)(2,1)} %param.7), channel_id=2, replica_groups=mesh['section'=2,'ctx'=4,'mp'=4] {'ctx'}, dimensions={1}, use_global_device_ids=true | all-gather | bytes 655360 | tf_op jit(solution)/shard_map/all_gather | solution.py:27
  22.9 1.0 fusion.75
  23.9 1.1 fusion.76
  25.0 0.0 copy-done.1
  25.0 0.0 copy-start.3
  25.0 0.3 fusion.77
  25.3 0.4 fusion.78
  25.7 0.3 fusion.79
  25.9 0.4 fusion.80
  26.3 0.3 fusion.81
  26.6 0.4 fusion.82
  26.9 0.0 copy-done.3
  26.9 11.9 %all-gather.1 = bf16[1,512,512]{2,1,0:T(8,128)(2,1)S(1)} all-gather(bf16[1,128,512]{2,1,0:T(8,128)(2,1)S(1)} %copy-done.3), channel_id=3, replica_groups=mesh['section'=2,'ctx'=4,'mp'=4] {'ctx'}, dimensions={1}, use_global_device_ids=true | all-gather | bytes 655360 | tf_op jit(solution)/shard_map/all_gather | solution.py:28
  38.8 0.2 fusion.11
  39.0 0.3 constant_dynamic-update-slice_fusion.7
  39.3 0.2 fusion.13
  39.5 0.3 constant_dynamic-update-slice_fusion.6
  39.8 0.2 fusion.15
  40.0 0.3 constant_dynamic-update-slice_fusion.5
  40.2 0.2 fusion.17
  40.4 0.3 constant_dynamic-update-slice_fusion.4
  40.7 0.2 fusion.19
  40.9 0.3 constant_dynamic-update-slice_fusion.3
  41.2 0.2 fusion.21
  41.4 0.3 constant_dynamic-update-slice_fusion.2
  41.7 0.2 fusion.23
  41.9 0.3 constant_dynamic-update-slice_fusion.1
  42.1 0.2 fusion.25
  42.3 0.3 constant_dynamic-update-slice_fusion
  42.6 11.8 %all_gather.11 = bf16[512,512]{0,1:T(8,128)(2,1)S(1)} all-gather(bf16[128,512]{0,1:T(8,128)(2,1)S(1)} %get-tuple-element.36), channel_id=1, replica_groups=mesh['section'=2,'ctx'=4,'mp'=4] {'ctx'}, dimensions={0}, use_global_device_ids=true | all-gather | bytes 655360 | tf_op jit(solution)/shard_map/all_gather | solution.py:46
  54.5 0.0 copy-done
  54.5 0.8 fusion
  55.3 0.2 copy.13
  55.5 29.8 %all_to_all.19 = bf16[4,128,1168]{1,2,0:T(8,128)(2,1)} all-to-all(bf16[4,128,1168]{1,2,0:T(8,128)(2,1)S(1)} %bitcast.37), channel_id=1, replica_groups=mesh['section'=2,'ctx'=4,'mp'=4] {'ctx'}, dimensions={0} | all-to-all | bytes 2392064 | tf_op jit(solution)/shard_map/all_to_all | solution.py:50
  85.3 0.0 copy-start.2
  85.3 0.0 reduce-scatter.4.cloned.1.call-update
  85.4 32.1 %reduce-scatter.4.cloned.1.call-done = bf16[128,1168]{0,1:T(8,128)(2,1)} async-done(((bf16[128,4672]{0,1:T(8,128)(2,1)}), bf16[128,1168]{0,1:T(8,128)(2,1)}) %reduce-scatter.4.cloned.1.call-update) | async-done | bytes 299024
  117.5 0.0 copy-done.2
  117.5 1.0 fusion.10
  118.6 0.7 collective-permute-start
  119.3 0.8 copy.10
  120.1 0.4 collective-permute-done
  120.5 0.7 copy.29
  (8 shorter events, 0.1 us)
Async XLA Ops:
  7.2 47.3 %copy-start = (bf16[1,1168,512]{2,1,0:T(8,128)(2,1)S(1)}, bf16[1,1168,512]{2,1,0:T(8,128)(2,1)}, u32[]{:S(2)}) copy-start(bf16[1,1168,512]{2,1,0:T(8,128)(2,1)} %param.9) | copy-start | bytes 3588100
  7.2 17.8 %copy-start.1 = (bf16[1,128,512]{2,1,0:T(8,128)(2,1)S(1)}, bf16[1,128,512]{2,1,0:T(8,128)(2,1)}, u32[]{:S(2)}) copy-start(bf16[1,128,512]{2,1,0:T(8,128)(2,1)} %param.6) | copy-start | bytes 393220
  7.2 110.3 %reduce-scatter.4.cloned.1.call-start = ((), (), s32[]{:S(2)}) async-start(), calls=%async_computation.2 | async-start | bytes 1495040
  25.0 1.9 %copy-start.3 = (bf16[1,128,512]{2,1,0:T(8,128)(2,1)S(1)}, bf16[1,128,512]{2,1,0:T(8,128)(2,1)}, u32[]{:S(2)}) copy-start(bf16[1,128,512]{2,1,0:T(8,128)(2,1)} %param.8) | copy-start | bytes 393220
  85.3 32.2 %copy-start.2 = (bf16[1,128,1168]{1,2,0:T(8,128)(2,1)S(1)}, bf16[1,128,1168]{1,2,0:T(8,128)(2,1)}, u32[]{:S(2)}) copy-start(bf16[1,128,1168]{1,2,0:T(8,128)(2,1)} %param.5) | copy-start | bytes 897028
  118.6 2.0 %collective-permute-start = (bf16[128,1168]{0,1:T(8,128)(2,1)S(1)}, bf16[128,1168]{0,1:T(8,128)(2,1)S(1)}, u32[]{:S(2)}, u32[]{:S(2)}) collective-permute-start(bf16[128,1168]{0,1:T(8,128)(2,1)S(1)} %fusion.10), channel_id=1, source_target_pairs={{16,0},{0,16},{17,1},{1,17},{18,2},{2,18},{19,3},{3,19},{20,4},{4,... | collective-permute-start | bytes 897032 | tf_op jit(solution)/shard_map/ppermute | solution.py:12
Sparse Core Ops, SparseCore 0:
  85.4 32.0 reduce-scatter.3
where the time goes:
time: 129 us; the launch traced here: 128 us
  blocking collectives  69.2 us (54%)
  waiting for transfers between devices  32.6 us (25%)
  between operations  14.1 us (11%)
  matrix products  7.04 us (5%)
  other arithmetic  2.6 us (2%)
  local copies, waits for them, and re-layouts  1.78 us (1%)
    unnamed x2, waiting for transfers between devices  32.2 us
    all_to_all x1, blocking collectives, body(): lax.all_to_all(projected, 'ctx', split_axis=0, concat_axis=1, tiled=True)  29.8 us
    all_gather x1, blocking collectives, body(): lax.all_gather(keys_local, 'ctx', axis=0, tiled=True)  15.6 us
    all_gather x1, blocking collectives, body(): lax.all_gather(values_local, 'ctx', axis=0, tiled=True)  11.9 us
    all_gather x1, blocking collectives, body(): context_all = lax.all_gather(context, 'ctx', axis=0, tiled=True)  11.8 us
    dot_general x8, matrix products, head_scores(): jnp.einsum('qd,kd->qk', query_h, keys_h, preferred_element_type=jnp.float32)  4.01 us
  transfers between devices with their start and end apart: 2, of which 2 were waited for; matrix products, arithmetic and copies ran while one was open for 1% of the time, Pallas kernels for 0%

commit v1 on v0

--- a/solution.py
+++ b/solution.py
@@ -1,9 +1,285 @@
+import functools
+
 import jax
 import jax.numpy as jnp
 from jax import lax
+from jax.experimental import pallas as pl
+from jax.experimental.pallas import tpu as pltpu
 from jax.sharding import PartitionSpec as P
 
 HEAD_DIM = 64
+MESH = pl.DeviceIdType.MESH
+NT = (((1,), (1,)), ((), ()))
+
+
+def dot(a, b, dims=(((1,), (0,)), ((), ()))):
+    return lax.dot_general(a, b, dims, preferred_element_type=jnp.float32)
+
+
+def relay_kernel(
+    n,
+    order,
+    q_hbm,
+    k_hbm,
+    v_hbm,
+    w_hbm,
+    hid_hbm,
+    branch_out,
+    hid_out,
+    ctx_out,
+    qkv,
+    w,
+    expo,
+    total,
+    ctx,
+    part,
+    red,
+    zsrc,
+    zin,
+    local_sem,
+    qkv_send,
+    qkv_recv,
+    hid_sem,
+    ctx_send,
+    ctx_recv,
+    red_send,
+    red_recv,
+    z_send,
+    z_recv,
+    out_send,
+    out_recv,
+):
+    s = lax.axis_index("section")
+    c = lax.axis_index("ctx")
+    m = lax.axis_index("mp")
+    other = 1 - s
+    wide = ctx.shape[2] // n
+    rows = ctx.shape[1]
+    cut = rows // n
+
+    def columns(j):
+        return pl.ds(pl.multiple_of(j * wide, wide), wide)
+
+    def send(src, dst, send_sem, recv_sem, device):
+        copy = pltpu.make_async_remote_copy(
+            src_ref=src,
+            dst_ref=dst,
+            send_sem=send_sem,
+            recv_sem=recv_sem,
+            device_id=device,
+            device_id_type=MESH,
+        )
+        copy.start()
+        return copy
+
+    inputs = (k_hbm, q_hbm, v_hbm)
+    own = []
+    for i, ref in enumerate(inputs):
+        own.append(pltpu.make_async_copy(ref.at[:, columns(c)], qkv.at[i, c], local_sem.at[i]))
+    own.append(pltpu.make_async_copy(w_hbm, w, local_sem.at[3]))
+    for copy in own:
+        copy.start()
+
+    barrier = pltpu.get_barrier_semaphore()
+    for d in range(1, n):
+        pl.semaphore_signal(barrier, inc=1, device_id=(s, lax.rem(c + d, n), m), device_id_type=MESH)
+        pl.semaphore_signal(barrier, inc=1, device_id=(s, c, lax.rem(m + d, n)), device_id_type=MESH)
+    for a in range(n):
+        pl.semaphore_signal(barrier, inc=1, device_id=(other, c, a), device_id_type=MESH)
+    pl.semaphore_wait(barrier, 3 * n - 2)
+
+    qkv_copies = []
+    for i, ref in enumerate(inputs):
+        group = []
+        for d in range(1, n):
+            j = lax.rem(c + d, n)
+            group.append(
+                send(ref.at[:, columns(j)], qkv.at[i, c], qkv_send.at[i, d - 1], qkv_recv.at[i, d - 1], (s, j, m))
+            )
+        qkv_copies.append(group)
+    hid_copy = send(hid_hbm, hid_out, hid_sem.at[0], hid_sem.at[1], (other, c, m))
+
+    lane = lax.broadcasted_iota(jnp.int32, (rows, wide), 1) // HEAD_DIM
+    heads = wide // HEAD_DIM
+    masks = [jnp.where(lane == h, 1.0, 0.0).astype(jnp.bfloat16) for h in range(heads)]
+    for i in (0, 1):
+        own[i].wait()
+        for copy in qkv_copies[i]:
+            copy.wait_recv()
+    keys_all = qkv[0].reshape(n * rows, wide)
+    for r in order:
+        q_r = qkv[1, r]
+        scores = dot(jnp.concatenate([q_r * mask for mask in masks], axis=0), keys_all, NT)
+        e = jnp.exp(scores - jnp.max(scores, axis=1, keepdims=True))
+        sums = jnp.sum(e, axis=1, keepdims=True)
+        wide_sum = jnp.broadcast_to(sums[:rows], (rows, wide))
+        for h in range(1, heads):
+            wide_sum = jnp.where(lane == h, sums[h * rows : (h + 1) * rows], wide_sum)
+        total[r] = wide_sum
+        expo[r] = e.astype(jnp.bfloat16)
+
+    own[2].wait()
+    for copy in qkv_copies[2]:
+        copy.wait_recv()
+    values_all = qkv[2].reshape(n * rows, wide)
+    ctx_copies = {}
+    for r in order:
+        both = dot(expo[r], values_all)
+        picked = both[:rows]
+        for h in range(1, heads):
+            picked = jnp.where(lane == h, both[h * rows : (h + 1) * rows], picked)
+        ctx[r, :, columns(c)] = (picked / total[r]).astype(jnp.bfloat16)
+        ctx_copies[r] = [
+            send(
+                ctx.at[r, :, columns(c)],
+                ctx.at[r, :, columns(c)],
+                ctx_send.at[r, d - 1],
+                ctx_recv.at[r, d - 1],
+                (s, lax.rem(c + d, n), m),
+            )
+            for d in range(1, n)
+        ]
+
+    own[3].wait()
+    red_copies = {}
+
+    def project(r):
+        for copy in ctx_copies[r]:
+            copy.wait_recv()
+        part[r] = dot(ctx[r], w[...], NT).astype(jnp.bfloat16).reshape(part.shape[1:])
+        group = []
+        for d in range(1, n):
+            t = lax.rem(m + d, n)
+            group.append(
+                send(part.at[r, t], red.at[r, d - 1], red_send.at[r, d - 1], red_recv.at[r, d - 1], (s, c, t))
+            )
+        red_copies[r] = group
+
+    def z_copy(r):
+        return pltpu.make_async_remote_copy(
+            src_ref=zsrc.at[r],
+            dst_ref=zin.at[c],
+            send_sem=z_send.at[r],
+            recv_sem=z_recv.at[c],
+            device_id=(s, r, m),
+            device_id_type=MESH,
+        )
+
+    def reduce(r):
+        for copy in red_copies[r]:
+            copy.wait_recv()
+        acc = part[r, m].astype(jnp.float32)
+        for d in range(1, n):
+            acc = acc + red[r, d - 1].astype(jnp.float32)
+        acc = acc.astype(jnp.bfloat16)
+
+        @pl.when(c == r)
+        def _():
+            zin[c] = acc
+
+        @pl.when(c != r)
+        def _():
+            zsrc[r] = acc
+            z_copy(r).start()
+
+    project(order[0])
+    for i in range(1, n):
+        project(order[i])
+        reduce(order[i - 1])
+    ctx_back = pltpu.make_async_copy(ctx.at[c], ctx_out, local_sem.at[4])
+    ctx_back.start()
+    reduce(order[n - 1])
+
+    out_copies = []
+    for step in range(n):
+        a = lax.rem(c + step, n)
+        if step:
+            pltpu.make_async_remote_copy(
+                src_ref=zsrc.at[0],
+                dst_ref=zin.at[a],
+                send_sem=z_send.at[0],
+                recv_sem=z_recv.at[a],
+                device_id=(s, a, m),
+                device_id_type=MESH,
+            ).wait_recv()
+        out_copies.append(
+            send(
+                zin.at[a],
+                branch_out.at[pl.ds(pl.multiple_of(m * cut, cut), cut)],
+                out_send.at[step],
+                out_recv.at[m],
+                (other, c, a),
+            )
+        )
+
+    ctx_back.wait()
+    for group in qkv_copies + list(ctx_copies.values()) + list(red_copies.values()):
+        for copy in group:
+            copy.wait_send()
+    hid_copy.wait()
+    for r in range(n):
+        pl.when(c != r)(z_copy(r).wait_send)
+    for copy in out_copies:
+        copy.wait_send()
+    for g in range(n):
+        pltpu.make_async_remote_copy(
+            src_ref=zin.at[0],
+            dst_ref=branch_out.at[pl.ds(g * cut, cut)],
+            send_sem=out_send.at[0],
+            recv_sem=out_recv.at[g],
+            device_id=(other, c, g),
+            device_id_type=MESH,
+        ).wait_recv()
+
+
+def relay_body(n, hidden, query, keys, values, w_out):
+    rows, inner = query.shape[1:]
+    depth = hidden.shape[2]
+    wide = inner // n
+    heads = wide // HEAD_DIM
+    cut = rows // n
+    order = sorted(range(n), key=lambda r: (-abs(2 * r - n + 1), r))
+    bf16 = jnp.bfloat16
+    dma = pltpu.SemaphoreType.DMA
+    any_spec = pl.BlockSpec(memory_space=pl.ANY)
+    branch, carried, context = pl.pallas_call(
+        functools.partial(relay_kernel, n, order),
+        out_shape=(
+            jax.ShapeDtypeStruct((rows, depth), bf16),
+            jax.ShapeDtypeStruct((rows, depth), bf16),
+            jax.ShapeDtypeStruct((rows, inner), bf16),
+        ),
+        in_specs=[any_spec] * 5,
+        out_specs=(any_spec,) * 3,
+        scratch_shapes=[
+            pltpu.VMEM((3, n, rows, wide), bf16),
+            pltpu.VMEM((depth, inner), bf16),
+            pltpu.VMEM((n, heads * rows, n * rows), bf16),
+            pltpu.VMEM((n, rows, wide), jnp.float32),
+            pltpu.VMEM((n, rows, inner), bf16),
+            pltpu.VMEM((n, n, cut, depth), bf16),
+            pltpu.VMEM((n, n - 1, cut, depth), bf16),
+            pltpu.VMEM((n, cut, depth), bf16),
+            pltpu.VMEM((n, cut, depth), bf16),
+            dma((5,)),
+            dma((3, n - 1)),
+            dma((3, n - 1)),
+            dma((2,)),
+            dma((n, n - 1)),
+            dma((n, n - 1)),
+            dma((n, n - 1)),
+            dma((n, n - 1)),
+            dma((n,)),
+            dma((n,)),
+            dma((n,)),
+            dma((n,)),
+        ],
+        compiler_params=pltpu.CompilerParams(
+            collective_id=0, has_side_effects=True, vmem_limit_bytes=32 * 2**20
+        ),
+    )(query[0], keys[0], values[0], w_out[0], hidden[0])
+    handed = (carried.astype(jnp.float32) + branch.astype(jnp.float32)).astype(bf16)
+    return (handed[None], context[None])
 
 
 def from_behind(block, axis, distance):
@@ -17,6 +293,10 @@
 
 
 def body(hidden, query, keys, values, w_out):
+    n = lax.axis_size("ctx")
+    square = lax.axis_size("mp") == n and lax.axis_size("section") == 2
+    if square and query.shape[2] % (128 * n) == 0 and query.shape[1] % (16 * n) == 0:
+        return relay_body(n, hidden, query, keys, values, w_out)
     rows = hidden[0]
     query_rows = query[0]
     inner_dev = query_rows.shape[1]

time: 129 us -> 54.4 us (0.42)
  the two profiles are of different devices: /device:TPU:1 before, /device:TPU:17 now
where the time goes in v1:
time: 54.4 us; the launch traced here: 54.2 us
  Pallas kernels  46.8 us (86%)
  local copies, waits for them, and re-layouts  6.66 us (12%)
  between operations  0.66 us (1%)
    pallas_call x1, Pallas kernels, relay_body(): pl.pallas_call(functools.partial(relay_kernel, n, order), out_shape=(jax....  46.8 us
    unnamed x11, local copies, waits for them, and re-layouts  6.66 us

profile of v1, /device:TPU:17, one launch (start us, length us, event | category | flops | bytes accessed | tf_op | source)
XLA Modules:
  0.0 54.2 jit_solution(7399306558108364467)
XLA Ops:
  0.6 1.1 %copy.7 = bf16[1,128,1168]{2,1,0:T(8,128)(2,1)S(1)} copy(bf16[1,128,1168]{1,2,0:T(8,128)(2,1)} %param.5) | data formatting | bytes 598016 | tf_op args[0]
  1.8 0.0 copy-start
  1.8 1.3 %copy-done = bf16[1,1168,512]{2,1,0:T(8,128)(2,1)S(1)} copy-done((bf16[1,1168,512]{2,1,0:T(8,128)(2,1)S(1)}, bf16[1,1168,512]{2,1,0:T(8,128)(2,1)}, u32[]{:S(2)}) %copy-start) | copy-done | bytes 1196056
  3.0 0.0 copy-start.1
  3.0 0.9 %copy-done.1 = bf16[1,128,512]{2,1,0:T(8,128)(2,1)S(1)} copy-done((bf16[1,128,512]{2,1,0:T(8,128)(2,1)S(1)}, bf16[1,128,512]{2,1,0:T(8,128)(2,1)}, u32[]{:S(2)}) %copy-start.1) | copy-done | bytes 131096
  3.9 0.0 copy-start.2
  4.0 0.9 %copy-done.2 = bf16[1,128,512]{2,1,0:T(8,128)(2,1)S(1)} copy-done((bf16[1,128,512]{2,1,0:T(8,128)(2,1)S(1)}, bf16[1,128,512]{2,1,0:T(8,128)(2,1)}, u32[]{:S(2)}) %copy-start.2) | copy-done | bytes 131096
  4.9 0.0 copy-start.3
  4.9 0.9 %copy-done.3 = bf16[1,128,512]{2,1,0:T(8,128)(2,1)S(1)} copy-done((bf16[1,128,512]{2,1,0:T(8,128)(2,1)S(1)}, bf16[1,128,512]{2,1,0:T(8,128)(2,1)}, u32[]{:S(2)}) %copy-start.3) | copy-done | bytes 131096
  5.8 46.8 %shard_map.68 = (bf16[128,1168]{1,0:T(8,128)(2,1)S(1)}, bf16[128,1168]{1,0:T(8,128)(2,1)S(1)}, bf16[128,512]{1,0:T(8,128)(2,1)S(1)}) custom-call(bf16[128,512]{1,0:T(8,128)(2,1)S(1)} %bitcast.11, bf16[128,512]{1,0:T(8,128)(2,1)S(1)} %bitcast.12, bf16[128,512]{1,0:T(8,128)(2,1)S(1)} %bitcast.13, bf16[1168,512]{1,0:T(8,128)(2,1)S(1)} %bitcast.9, ...), custom_call_target="tpu_custom_call" | custom-call | tf_op jit(solution)/shard_map/pallas_call | solution.py:245
  52.5 0.1 fusion
  52.6 0.9 %copy.8 = bf16[1,128,1168]{1,2,0:T(8,128)(2,1)} copy(bf16[1,128,1168]{2,1,0:T(8,128)(2,1)S(1)} %fusion) | data formatting | bytes 598016
  53.5 0.7 %copy.10 = bf16[1,128,512]{2,1,0:T(8,128)(2,1)} copy(bf16[1,128,512]{2,1,0:T(8,128)(2,1)S(1)} %bitcast.10) | data formatting | bytes 262144
Async XLA Ops:
  1.8 1.3 %copy-start = (bf16[1,1168,512]{2,1,0:T(8,128)(2,1)S(1)}, bf16[1,1168,512]{2,1,0:T(8,128)(2,1)}, u32[]{:S(2)}) copy-start(bf16[1,1168,512]{2,1,0:T(8,128)(2,1)} %param.9) | copy-start | bytes 3588100
  3.0 0.9 %copy-start.1 = (bf16[1,128,512]{2,1,0:T(8,128)(2,1)S(1)}, bf16[1,128,512]{2,1,0:T(8,128)(2,1)}, u32[]{:S(2)}) copy-start(bf16[1,128,512]{2,1,0:T(8,128)(2,1)} %param.6) | copy-start | bytes 393220
  3.9 0.9 %copy-start.2 = (bf16[1,128,512]{2,1,0:T(8,128)(2,1)S(1)}, bf16[1,128,512]{2,1,0:T(8,128)(2,1)}, u32[]{:S(2)}) copy-start(bf16[1,128,512]{2,1,0:T(8,128)(2,1)} %param.7) | copy-start | bytes 393220
  4.9 0.9 %copy-start.3 = (bf16[1,128,512]{2,1,0:T(8,128)(2,1)S(1)}, bf16[1,128,512]{2,1,0:T(8,128)(2,1)}, u32[]{:S(2)}) copy-start(bf16[1,128,512]{2,1,0:T(8,128)(2,1)} %param.8) | copy-start | bytes 393220

commit v2 on v1

--- a/solution.py
+++ b/solution.py
@@ -55,7 +55,8 @@
     other = 1 - s
     wide = ctx.shape[2] // n
     rows = ctx.shape[1]
-    cut = rows // n
+    depth = w_hbm.shape[0]
+    cut = zsrc.shape[1]
 
     def columns(j):
         return pl.ds(pl.multiple_of(j * wide, wide), wide)
@@ -76,9 +77,12 @@
     own = []
     for i, ref in enumerate(inputs):
         own.append(pltpu.make_async_copy(ref.at[:, columns(c)], qkv.at[i, c], local_sem.at[i]))
-    own.append(pltpu.make_async_copy(w_hbm, w, local_sem.at[3]))
+    own.append(pltpu.make_async_copy(w_hbm, w.at[pl.ds(0, depth)], local_sem.at[3]))
     for copy in own:
         copy.start()
+
+    if n * cut > depth:
+        w[depth:] = jnp.zeros((n * cut - depth, w.shape[1]), w.dtype)
 
     barrier = pltpu.get_barrier_semaphore()
     for d in range(1, n):
@@ -146,7 +150,7 @@
     def project(r):
         for copy in ctx_copies[r]:
             copy.wait_recv()
-        part[r] = dot(ctx[r], w[...], NT).astype(jnp.bfloat16).reshape(part.shape[1:])
+        part[r] = dot(w[...], ctx[r], NT).astype(jnp.bfloat16).reshape(part.shape[1:])
         group = []
         for d in range(1, n):
             t = lax.rem(m + d, n)
@@ -237,30 +241,30 @@
     depth = hidden.shape[2]
     wide = inner // n
     heads = wide // HEAD_DIM
-    cut = rows // n
+    cut = -(-depth // (16 * n)) * 16
     order = sorted(range(n), key=lambda r: (-abs(2 * r - n + 1), r))
     bf16 = jnp.bfloat16
     dma = pltpu.SemaphoreType.DMA
-    any_spec = pl.BlockSpec(memory_space=pl.ANY)
+    hbm = pl.BlockSpec(memory_space=pltpu.HBM)
     branch, carried, context = pl.pallas_call(
         functools.partial(relay_kernel, n, order),
         out_shape=(
-            jax.ShapeDtypeStruct((rows, depth), bf16),
-            jax.ShapeDtypeStruct((rows, depth), bf16),
+            jax.ShapeDtypeStruct((n * cut, rows), bf16),
+            jax.ShapeDtypeStruct((depth, rows), bf16),
             jax.ShapeDtypeStruct((rows, inner), bf16),
         ),
-        in_specs=[any_spec] * 5,
-        out_specs=(any_spec,) * 3,
+        in_specs=[hbm] * 5,
+        out_specs=(hbm,) * 3,
         scratch_shapes=[
             pltpu.VMEM((3, n, rows, wide), bf16),
-            pltpu.VMEM((depth, inner), bf16),
+            pltpu.VMEM((n * cut, inner), bf16),
             pltpu.VMEM((n, heads * rows, n * rows), bf16),
             pltpu.VMEM((n, rows, wide), jnp.float32),
             pltpu.VMEM((n, rows, inner), bf16),
-            pltpu.VMEM((n, n, cut, depth), bf16),
-            pltpu.VMEM((n, n - 1, cut, depth), bf16),
-            pltpu.VMEM((n, cut, depth), bf16),
-            pltpu.VMEM((n, cut, depth), bf16),
+            pltpu.VMEM((n, n, cut, rows), bf16),
+            pltpu.VMEM((n, n - 1, cut, rows), bf16),
+            pltpu.VMEM((n, cut, rows), bf16),
+            pltpu.VMEM((n, cut, rows), bf16),
             dma((5,)),
             dma((3, n - 1)),
             dma((3, n - 1)),
@@ -275,11 +279,11 @@
             dma((n,)),
         ],
         compiler_params=pltpu.CompilerParams(
-            collective_id=0, has_side_effects=True, vmem_limit_bytes=32 * 2**20
+            collective_id=0, has_side_effects=True, vmem_limit_bytes=60 * 2**20
         ),
-    )(query[0], keys[0], values[0], w_out[0], hidden[0])
-    handed = (carried.astype(jnp.float32) + branch.astype(jnp.float32)).astype(bf16)
-    return (handed[None], context[None])
+    )(query[0], keys[0], values[0], w_out[0], hidden[0].T)
+    handed = (carried.astype(jnp.float32) + branch[:depth].astype(jnp.float32)).astype(bf16)
+    return (handed.T[None], context[None])
 
 
 def from_behind(block, axis, distance):
@@ -295,7 +299,7 @@
 def body(hidden, query, keys, values, w_out):
     n = lax.axis_size("ctx")
     square = lax.axis_size("mp") == n and lax.axis_size("section") == 2
-    if square and query.shape[2] % (128 * n) == 0 and query.shape[1] % (16 * n) == 0:
+    if square and query.shape[2] % (128 * n) == 0 and query.shape[1] % 128 == 0:
         return relay_body(n, hidden, query, keys, values, w_out)
     rows = hidden[0]
     query_rows = query[0]

time: 54.4 us -> 50.7 us (0.932)
  local copies, waits for them, and re-layouts: 6.66 us -> 1.57 us
  other arithmetic: 0.08 us -> 1.85 us
    unnamed x11 -> x1, local copies, waits for them, and re-layouts: 6.66 us -> 1.57 us
    broadcast_in_dim x1, other arithmetic: 0.08 us -> 1.85 us  [relay_body(): return (handed.T[None], context[None])]
where the time goes in v2:
time: 50.7 us; the launch traced here: 50.5 us
  Pallas kernels  46.5 us (92%)
  other arithmetic  1.85 us (4%)
  local copies, waits for them, and re-layouts  1.57 us (3%)
  between operations  0.64 us (1%)
    pallas_call x1, Pallas kernels, relay_body(): pl.pallas_call(functools.partial(relay_kernel, n, order), out_shape=(jax....  46.5 us
    broadcast_in_dim x1, other arithmetic, relay_body(): return (handed.T[None], context[None])  1.85 us
    unnamed x1, local copies, waits for them, and re-layouts  1.57 us

profile of v2, /device:TPU:17, one launch (start us, length us, event | category | flops | bytes accessed | tf_op | source)
XLA Modules:
  0.0 50.5 jit_solution(14843375737637301338)
XLA Ops:
  0.6 46.5 %shard_map.68 = (bf16[1216,128]{1,0:T(8,128)(2,1)}, bf16[1168,128]{1,0:T(8,128)(2,1)}, bf16[128,512]{1,0:T(8,128)(2,1)}) custom-call(bf16[128,512]{1,0:T(8,128)(2,1)} %bitcast.14, bf16[128,512]{1,0:T(8,128)(2,1)} %bitcast.15, bf16[128,512]{1,0:T(8,128)(2,1)} %bitcast.16, bf16[1168,512]{1,0:T(8,128)(2,1)} %bitcast.12, bf16[1168,128]{1,0:T(8,128)(2,1)} %bitcast.13), custom_call_target="tpu_custom_call" | custom-call | tf_op jit(solution)/shard_map/pallas_call | solution.py:249
  47.1 1.8 %fusion = bf16[1,128,1168]{1,2,0:T(8,128)(2,1)} fusion(bf16[1168,128]{1,0:T(8,128)(2,1)} %get-tuple-element.5, bf16[1216,128]{1,0:T(8,128)(2,1)} %get-tuple-element.6), kind=kLoop, calls=%fused_computation.1 | loop fusion | flops 598016 | bytes 897024 | tf_op jit(solution)/shard_map/broadcast_in_dim | solution.py:286
  48.9 1.6 %copy.8 = bf16[1,128,512]{2,1,0:T(8,128)(2,1)} copy(bf16[1,128,512]{2,1,0:T(8,128)(2,1)} %bitcast.17) | data formatting | bytes 262144

commit v3 on v2

--- a/solution.py
+++ b/solution.py
@@ -126,30 +126,57 @@
     for copy in qkv_copies[2]:
         copy.wait_recv()
     values_all = qkv[2].reshape(n * rows, wide)
-    ctx_copies = {}
-    for r in order:
+
+    relayed = (n - 1) * (2 - c)
+
+    def ctx_copy(r, source, target, slot):
+        return pltpu.make_async_remote_copy(
+            src_ref=ctx.at[r, :, columns(source)],
+            dst_ref=ctx.at[r, :, columns(source)],
+            send_sem=ctx_send.at[r, slot],
+            recv_sem=ctx_recv.at[r, source],
+            device_id=(s, target, m),
+            device_id_type=MESH,
+        )
+
+    def ctx_peers():
+        for d in range(1, n):
+            j = lax.rem(c + d, n)
+            yield d - 1, j, jnp.abs(j - c) < n - 1
+
+    def when(condition, action):
+        @pl.when(condition)
+        def _():
+            action()
+
+    def attend(r):
         both = dot(expo[r], values_all)
         picked = both[:rows]
         for h in range(1, heads):
             picked = jnp.where(lane == h, both[h * rows : (h + 1) * rows], picked)
         ctx[r, :, columns(c)] = (picked / total[r]).astype(jnp.bfloat16)
-        ctx_copies[r] = [
-            send(
-                ctx.at[r, :, columns(c)],
-                ctx.at[r, :, columns(c)],
-                ctx_send.at[r, d - 1],
-                ctx_recv.at[r, d - 1],
-                (s, lax.rem(c + d, n), m),
-            )
-            for d in range(1, n)
-        ]
-
-    own[3].wait()
+        for slot, j, direct in ctx_peers():
+            when(direct, lambda: ctx_copy(r, c, j, slot).start())
+
+    def ctx_arrive(r):
+        @pl.when((c > 0) & (c < n - 1))
+        def _():
+            passing = ctx_copy(r, relayed, n - 1 - relayed, n - 1)
+            passing.wait_recv()
+            passing.start()
+
+        for _, j, _ in ctx_peers():
+            when(j != relayed, lambda: ctx_copy(r, j, j, 0).wait_recv())
+
+    def ctx_sent(r):
+        for slot, j, direct in ctx_peers():
+            when(direct, lambda: ctx_copy(r, c, j, slot).wait_send())
+        when((c > 0) & (c < n - 1), lambda: ctx_copy(r, relayed, n - 1 - relayed, n - 1).wait_send())
+
     red_copies = {}
 
     def project(r):
-        for copy in ctx_copies[r]:
-            copy.wait_recv()
+        ctx_arrive(r)
         part[r] = dot(w[...], ctx[r], NT).astype(jnp.bfloat16).reshape(part.shape[1:])
         group = []
         for d in range(1, n):
@@ -186,13 +213,18 @@
             zsrc[r] = acc
             z_copy(r).start()
 
-    project(order[0])
-    for i in range(1, n):
+    attend(order[0])
+    own[3].wait()
+    for i in range(n):
+        if i < n - 1:
+            attend(order[i + 1])
         project(order[i])
-        reduce(order[i - 1])
+        if i > 1:
+            reduce(order[i - 2])
     ctx_back = pltpu.make_async_copy(ctx.at[c], ctx_out, local_sem.at[4])
     ctx_back.start()
-    reduce(order[n - 1])
+    for r in order[-2:]:
+        reduce(r)
 
     out_copies = []
     for step in range(n):
@@ -217,11 +249,12 @@
         )
 
     ctx_back.wait()
-    for group in qkv_copies + list(ctx_copies.values()) + list(red_copies.values()):
+    for group in qkv_copies + list(red_copies.values()):
         for copy in group:
             copy.wait_send()
     hid_copy.wait()
     for r in range(n):
+        ctx_sent(r)
         pl.when(c != r)(z_copy(r).wait_send)
     for copy in out_copies:
         copy.wait_send()
@@ -269,8 +302,8 @@
             dma((3, n - 1)),
             dma((3, n - 1)),
             dma((2,)),
-            dma((n, n - 1)),
-            dma((n, n - 1)),
+            dma((n, n)),
+            dma((n, n)),
             dma((n, n - 1)),
             dma((n, n - 1)),
             dma((n,)),
@@ -299,7 +332,7 @@
 def body(hidden, query, keys, values, w_out):
     n = lax.axis_size("ctx")
     square = lax.axis_size("mp") == n and lax.axis_size("section") == 2
-    if square and query.shape[2] % (128 * n) == 0 and query.shape[1] % 128 == 0:
+    if square and n == 4 and query.shape[2] % (128 * n) == 0 and query.shape[1] % 128 == 0:
         return relay_body(n, hidden, query, keys, values, w_out)
     rows = hidden[0]
     query_rows = query[0]

time: 50.7 us -> 50.7 us (level)
  no operation moved by 1% of the time
where the time goes in v3:
time: 50.7 us; the launch traced here: 50.5 us
  Pallas kernels  46.5 us (92%)
  other arithmetic  1.85 us (4%)
  local copies, waits for them, and re-layouts  1.57 us (3%)
  between operations  0.64 us (1%)
    pallas_call x1, Pallas kernels, relay_body(): pl.pallas_call(functools.partial(relay_kernel, n, order), out_shape=(jax....  46.5 us
    broadcast_in_dim x1, other arithmetic, relay_body(): return (handed.T[None], context[None])  1.85 us
    unnamed x1, local copies, waits for them, and re-layouts  1.57 us

profile of v3, /device:TPU:17, one launch (start us, length us, event | category | flops | bytes accessed | tf_op | source)
XLA Modules:
  0.0 50.5 jit_solution(7876504882082842815)
XLA Ops:
  0.6 46.5 %shard_map.68 = (bf16[1216,128]{1,0:T(8,128)(2,1)}, bf16[1168,128]{1,0:T(8,128)(2,1)}, bf16[128,512]{1,0:T(8,128)(2,1)}) custom-call(bf16[128,512]{1,0:T(8,128)(2,1)} %bitcast.14, bf16[128,512]{1,0:T(8,128)(2,1)} %bitcast.15, bf16[128,512]{1,0:T(8,128)(2,1)} %bitcast.16, bf16[1168,512]{1,0:T(8,128)(2,1)} %bitcast.12, bf16[1168,128]{1,0:T(8,128)(2,1)} %bitcast.13), custom_call_target="tpu_custom_call" | custom-call | tf_op jit(solution)/shard_map/pallas_call | solution.py:282
  47.1 1.8 %fusion = bf16[1,128,1168]{1,2,0:T(8,128)(2,1)} fusion(bf16[1168,128]{1,0:T(8,128)(2,1)} %get-tuple-element.5, bf16[1216,128]{1,0:T(8,128)(2,1)} %get-tuple-element.6), kind=kLoop, calls=%fused_computation.1 | loop fusion | flops 598016 | bytes 897024 | tf_op jit(solution)/shard_map/broadcast_in_dim | solution.py:319
  49.0 1.6 %copy.8 = bf16[1,128,512]{2,1,0:T(8,128)(2,1)} copy(bf16[1,128,512]{2,1,0:T(8,128)(2,1)} %bitcast.17) | data formatting | bytes 262144

commit v4 on v2

--- a/solution.py
+++ b/solution.py
@@ -18,7 +18,7 @@
 
 def relay_kernel(
     n,
-    order,
+    shifts,
     q_hbm,
     k_hbm,
     v_hbm,
@@ -110,8 +110,10 @@
         own[i].wait()
         for copy in qkv_copies[i]:
             copy.wait_recv()
-    keys_all = qkv[0].reshape(n * rows, wide)
-    for r in order:
+
+    @pl.loop(0, n)
+    def _(r):
+        keys_all = qkv[0].reshape(n * rows, wide)
         q_r = qkv[1, r]
         scores = dot(jnp.concatenate([q_r * mask for mask in masks], axis=0), keys_all, NT)
         e = jnp.exp(scores - jnp.max(scores, axis=1, keepdims=True))
@@ -125,106 +127,96 @@
     own[2].wait()
     for copy in qkv_copies[2]:
         copy.wait_recv()
-    values_all = qkv[2].reshape(n * rows, wide)
-    ctx_copies = {}
-    for r in order:
+
+    @pl.loop(0, n)
+    def _(r):
+        values_all = qkv[2].reshape(n * rows, wide)
         both = dot(expo[r], values_all)
         picked = both[:rows]
         for h in range(1, heads):
             picked = jnp.where(lane == h, both[h * rows : (h + 1) * rows], picked)
         ctx[r, :, columns(c)] = (picked / total[r]).astype(jnp.bfloat16)
-        ctx_copies[r] = [
-            send(
-                ctx.at[r, :, columns(c)],
-                ctx.at[r, :, columns(c)],
-                ctx_send.at[r, d - 1],
-                ctx_recv.at[r, d - 1],
-                (s, lax.rem(c + d, n), m),
-            )
-            for d in range(1, n)
-        ]
-
+
+    def share(i):
+        group = []
+        for d in range(1, n):
+            j = lax.rem(c + d, n)
+            block = ctx.at[lax.rem(j + shifts[i], n), :, columns(c)]
+            group.append(send(block, block, ctx_send.at[i, d - 1], ctx_recv.at[i, d - 1], (s, j, m)))
+        ctx_copies.append(group)
+
+    ctx_copies = []
+    share(0)
+    share(1)
     own[3].wait()
-    red_copies = {}
-
-    def project(r):
-        for copy in ctx_copies[r]:
-            copy.wait_recv()
-        part[r] = dot(w[...], ctx[r], NT).astype(jnp.bfloat16).reshape(part.shape[1:])
+    red_copies = []
+
+    def project(i):
+        for d in range(1, n):
+            block = ctx.at[lax.rem(c + shifts[i], n), :, columns(lax.rem(c + d, n))]
+            pltpu.make_async_remote_copy(
+                src_ref=block,
+                dst_ref=block,
+                send_sem=ctx_send.at[i, d - 1],
+                recv_sem=ctx_recv.at[i, n - 1 - d],
+                device_id=(s, lax.rem(c + d, n), m),
+                device_id_type=MESH,
+            ).wait_recv()
+        r = lax.rem(c + shifts[i], n)
+        part[i] = dot(w[...], ctx[r], NT).astype(jnp.bfloat16).reshape(part.shape[1:])
         group = []
         for d in range(1, n):
             t = lax.rem(m + d, n)
             group.append(
-                send(part.at[r, t], red.at[r, d - 1], red_send.at[r, d - 1], red_recv.at[r, d - 1], (s, c, t))
+                send(part.at[i, t], red.at[i, d - 1], red_send.at[i, d - 1], red_recv.at[i, d - 1], (s, c, t))
             )
-        red_copies[r] = group
-
-    def z_copy(r):
-        return pltpu.make_async_remote_copy(
-            src_ref=zsrc.at[r],
-            dst_ref=zin.at[c],
-            send_sem=z_send.at[r],
-            recv_sem=z_recv.at[c],
-            device_id=(s, r, m),
-            device_id_type=MESH,
-        )
-
-    def reduce(r):
-        for copy in red_copies[r]:
+        red_copies.append(group)
+
+    z_copies = []
+
+    def reduce(i):
+        for copy in red_copies[i]:
             copy.wait_recv()
-        acc = part[r, m].astype(jnp.float32)
-        for d in range(1, n):
-            acc = acc + red[r, d - 1].astype(jnp.float32)
-        acc = acc.astype(jnp.bfloat16)
-
-        @pl.when(c == r)
-        def _():
-            zin[c] = acc
-
-        @pl.when(c != r)
-        def _():
-            zsrc[r] = acc
-            z_copy(r).start()
-
-    project(order[0])
-    for i in range(1, n):
-        project(order[i])
-        reduce(order[i - 1])
+        acc = part[i, m].astype(jnp.float32)
+        for d in range(1, n):
+            acc = acc + red[i, d - 1].astype(jnp.float32)
+        if shifts[i] == 0:
+            zin[i] = acc.astype(jnp.bfloat16)
+        else:
+            zsrc[i] = acc.astype(jnp.bfloat16)
+            target = lax.rem(c + shifts[i], n)
+            z_copies.append(send(zsrc.at[i], zin.at[i], z_send.at[i], z_recv.at[i], (s, target, m)))
+
+    out_copies = []
+
+    def hand_over(i):
+        if shifts[i]:
+            z_copies[i].wait_recv()
+        target = lax.rem(c + n - shifts[i], n)
+        piece = branch_out.at[pl.ds(pl.multiple_of(m * cut, cut), cut)]
+        out_copies.append(send(zin.at[i], piece, out_send.at[i], out_recv.at[m], (other, c, target)))
+
+    project(0)
+    for i in range(2, n):
+        share(i)
+        project(i - 1)
+        if i > 2:
+            reduce(i - 3)
+    project(n - 1)
     ctx_back = pltpu.make_async_copy(ctx.at[c], ctx_out, local_sem.at[4])
     ctx_back.start()
-    reduce(order[n - 1])
-
-    out_copies = []
-    for step in range(n):
-        a = lax.rem(c + step, n)
-        if step:
-            pltpu.make_async_remote_copy(
-                src_ref=zsrc.at[0],
-                dst_ref=zin.at[a],
-                send_sem=z_send.at[0],
-                recv_sem=z_recv.at[a],
-                device_id=(s, a, m),
-                device_id_type=MESH,
-            ).wait_recv()
-        out_copies.append(
-            send(
-                zin.at[a],
-                branch_out.at[pl.ds(pl.multiple_of(m * cut, cut), cut)],
-                out_send.at[step],
-                out_recv.at[m],
-                (other, c, a),
-            )
-        )
+    for i in range(n - 3, n):
+        reduce(i)
+        if i < n - 1:
+            hand_over(i - 1)
+    hand_over(n - 1)
+    hand_over(n - 2)
 
     ctx_back.wait()
-    for group in qkv_copies + list(ctx_copies.values()) + list(red_copies.values()):
+    for group in qkv_copies + ctx_copies + red_copies + [z_copies, out_copies]:
         for copy in group:
             copy.wait_send()
     hid_copy.wait()
-    for r in range(n):
-        pl.when(c != r)(z_copy(r).wait_send)
-    for copy in out_copies:
-        copy.wait_send()
     for g in range(n):
         pltpu.make_async_remote_copy(
             src_ref=zin.at[0],
@@ -242,12 +234,11 @@
     wide = inner // n
     heads = wide // HEAD_DIM
     cut = -(-depth // (16 * n)) * 16
-    order = sorted(range(n), key=lambda r: (-abs(2 * r - n + 1), r))
     bf16 = jnp.bfloat16
     dma = pltpu.SemaphoreType.DMA
     hbm = pl.BlockSpec(memory_space=pltpu.HBM)
     branch, carried, context = pl.pallas_call(
-        functools.partial(relay_kernel, n, order),
+        functools.partial(relay_kernel, n, (2, 1, 3, 0)),
         out_shape=(
             jax.ShapeDtypeStruct((n * cut, rows), bf16),
             jax.ShapeDtypeStruct((depth, rows), bf16),
@@ -282,8 +273,34 @@
             collective_id=0, has_side_effects=True, vmem_limit_bytes=60 * 2**20
         ),
     )(query[0], keys[0], values[0], w_out[0], hidden[0].T)
-    handed = (carried.astype(jnp.float32) + branch[:depth].astype(jnp.float32)).astype(bf16)
+    handed, context = pl.pallas_call(
+        finish_kernel,
+        out_shape=(
+            jax.ShapeDtypeStruct((depth, rows), bf16),
+            jax.ShapeDtypeStruct((rows, inner), bf16),
+        ),
+        in_specs=[hbm] * 3,
+        out_specs=(hbm,) * 2,
+        scratch_shapes=[pltpu.VMEM((depth, rows), bf16)] * 3 + [dma((4,))],
+        compiler_params=pltpu.CompilerParams(vmem_limit_bytes=60 * 2**20),
+    )(carried, branch, context)
     return (handed.T[None], context[None])
+
+
+def finish_kernel(carried, branch, context, handed, context_out, first, second, summed, sem):
+    depth = handed.shape[0]
+    kept = pltpu.make_async_copy(context, context_out, sem.at[0])
+    one = pltpu.make_async_copy(carried, first, sem.at[1])
+    two = pltpu.make_async_copy(branch.at[pl.ds(0, depth)], second, sem.at[2])
+    for copy in (one, two, kept):
+        copy.start()
+    one.wait()
+    two.wait()
+    summed[...] = (first[...].astype(jnp.float32) + second[...].astype(jnp.float32)).astype(jnp.bfloat16)
+    last = pltpu.make_async_copy(summed, handed, sem.at[3])
+    last.start()
+    last.wait()
+    kept.wait()
 
 
 def from_behind(block, axis, distance):
@@ -299,7 +316,7 @@
 def body(hidden, query, keys, values, w_out):
     n = lax.axis_size("ctx")
     square = lax.axis_size("mp") == n and lax.axis_size("section") == 2
-    if square and query.shape[2] % (128 * n) == 0 and query.shape[1] % 128 == 0:
+    if square and n == 4 and query.shape[2] % (128 * n) == 0 and query.shape[1] % 128 == 0:
         return relay_body(n, hidden, query, keys, values, w_out)
     rows = hidden[0]
     query_rows = query[0]

time: 50.7 us -> 50.4 us (level)
  the two profiles are of different devices: /device:TPU:17 before, /device:TPU:1 now
where the time goes in v4:
time: 50.4 us; the launch traced here: 50.2 us
  Pallas kernels  49.6 us (98%)
  between operations  0.64 us (1%)
    pallas_call x1, Pallas kernels, relay_body(): pl.pallas_call(functools.partial(relay_kernel, n, (2, 1, 3, 0)), out_shap...  44.5 us
    pallas_call x1, Pallas kernels, relay_body(): pl.pallas_call(finish_kernel, out_shape=(jax.ShapeDtypeStruct((depth, row...  5.11 us

profile of v4, /device:TPU:1, one launch (start us, length us, event | category | flops | bytes accessed | tf_op | source)
XLA Modules:
  0.0 50.2 jit_solution(12192831336177935898)
XLA Ops:
  0.6 44.5 %shard_map.68 = (bf16[1216,128]{1,0:T(8,128)(2,1)}, bf16[1168,128]{1,0:T(8,128)(2,1)}, bf16[128,512]{1,0:T(8,128)(2,1)}) custom-call(bf16[128,512]{1,0:T(8,128)(2,1)} %bitcast.13, bf16[128,512]{1,0:T(8,128)(2,1)} %bitcast.14, bf16[128,512]{1,0:T(8,128)(2,1)} %bitcast.15, bf16[1168,512]{1,0:T(8,128)(2,1)} %bitcast.11, bf16[1168,128]{1,0:T(8,128)(2,1)} %bitcast.12), custom_call_target="tpu_custom_call" | custom-call | tf_op jit(solution)/shard_map/pallas_call | solution.py:240
  45.1 5.1 %shard_map.69 = (bf16[1168,128]{1,0:T(8,128)(2,1)}, bf16[128,512]{1,0:T(8,128)(2,1)}) custom-call(bf16[1168,128]{1,0:T(8,128)(2,1)} %get-tuple-element.7.carried, bf16[1216,128]{1,0:T(8,128)(2,1)} %get-tuple-element.8.branch, bf16[128,512]{1,0:T(8,128)(2,1)} %get-tuple-element.9.context), custom_call_target="tpu_custom_call" | custom-call | tf_op jit(solution)/shard_map/pallas_call | solution.py:276

commit v5 on v4

--- a/solution.py
+++ b/solution.py
@@ -27,6 +27,8 @@
     branch_out,
     hid_out,
     ctx_out,
+    staged,
+    hid,
     qkv,
     w,
     expo,
@@ -74,10 +76,9 @@
         return copy
 
     inputs = (k_hbm, q_hbm, v_hbm)
-    own = []
-    for i, ref in enumerate(inputs):
-        own.append(pltpu.make_async_copy(ref.at[:, columns(c)], qkv.at[i, c], local_sem.at[i]))
+    own = [pltpu.make_async_copy(ref, staged.at[i], local_sem.at[i]) for i, ref in enumerate(inputs)]
     own.append(pltpu.make_async_copy(w_hbm, w.at[pl.ds(0, depth)], local_sem.at[3]))
+    own.append(pltpu.make_async_copy(hid_hbm, hid, local_sem.at[4]))
     for copy in own:
         copy.start()
 
@@ -93,21 +94,22 @@
     pl.semaphore_wait(barrier, 3 * n - 2)
 
     qkv_copies = []
-    for i, ref in enumerate(inputs):
+    for i in range(3):
+        own[i].wait()
         group = []
         for d in range(1, n):
             j = lax.rem(c + d, n)
             group.append(
-                send(ref.at[:, columns(j)], qkv.at[i, c], qkv_send.at[i, d - 1], qkv_recv.at[i, d - 1], (s, j, m))
+                send(staged.at[i, :, columns(j)], qkv.at[i, c], qkv_send.at[i, d - 1], qkv_recv.at[i, d - 1], (s, j, m))
             )
         qkv_copies.append(group)
-    hid_copy = send(hid_hbm, hid_out, hid_sem.at[0], hid_sem.at[1], (other, c, m))
+    for i in range(3):
+        qkv[i, c] = staged[i, :, columns(c)]
 
     lane = lax.broadcasted_iota(jnp.int32, (rows, wide), 1) // HEAD_DIM
     heads = wide // HEAD_DIM
     masks = [jnp.where(lane == h, 1.0, 0.0).astype(jnp.bfloat16) for h in range(heads)]
     for i in (0, 1):
-        own[i].wait()
         for copy in qkv_copies[i]:
             copy.wait_recv()
 
@@ -124,7 +126,6 @@
         total[r] = wide_sum
         expo[r] = e.astype(jnp.bfloat16)
 
-    own[2].wait()
     for copy in qkv_copies[2]:
         copy.wait_recv()
 
@@ -148,8 +149,20 @@
     ctx_copies = []
     share(0)
     share(1)
+    own[4].wait()
+    hid_copy = send(hid, hid_out, hid_sem.at[0], hid_sem.at[1], (other, c, m))
     own[3].wait()
-    red_copies = []
+
+    def red_copy(i, d):
+        t = lax.rem(m + d, n)
+        return pltpu.make_async_remote_copy(
+            src_ref=part.at[i, t],
+            dst_ref=red.at[i, d - 1],
+            send_sem=red_send.at[i, d - 1],
+            recv_sem=red_recv.at[i, d - 1],
+            device_id=(s, c, t),
+            device_id_type=MESH,
+        )
 
     def project(i):
         for d in range(1, n):
@@ -163,20 +176,22 @@
                 device_id_type=MESH,
             ).wait_recv()
         r = lax.rem(c + shifts[i], n)
-        part[i] = dot(w[...], ctx[r], NT).astype(jnp.bfloat16).reshape(part.shape[1:])
-        group = []
-        for d in range(1, n):
+
+        @pl.loop(1, n + 1)
+        def _(d):
             t = lax.rem(m + d, n)
-            group.append(
-                send(part.at[i, t], red.at[i, d - 1], red_send.at[i, d - 1], red_recv.at[i, d - 1], (s, c, t))
-            )
-        red_copies.append(group)
+            piece = w[pl.ds(pl.multiple_of(t * cut, cut), cut), :]
+            part[i, t] = dot(piece, ctx[r], NT).astype(jnp.bfloat16)
+
+            @pl.when(d < n)
+            def _():
+                red_copy(i, d).start()
 
     z_copies = []
 
     def reduce(i):
-        for copy in red_copies[i]:
-            copy.wait_recv()
+        for d in range(1, n):
+            red_copy(i, d).wait_recv()
         acc = part[i, m].astype(jnp.float32)
         for d in range(1, n):
             acc = acc + red[i, d - 1].astype(jnp.float32)
@@ -203,7 +218,7 @@
         if i > 2:
             reduce(i - 3)
     project(n - 1)
-    ctx_back = pltpu.make_async_copy(ctx.at[c], ctx_out, local_sem.at[4])
+    ctx_back = pltpu.make_async_copy(ctx.at[c], ctx_out, local_sem.at[5])
     ctx_back.start()
     for i in range(n - 3, n):
         reduce(i)
@@ -213,10 +228,13 @@
     hand_over(n - 2)
 
     ctx_back.wait()
-    for group in qkv_copies + ctx_copies + red_copies + [z_copies, out_copies]:
+    for group in qkv_copies + ctx_copies + [z_copies, out_copies]:
         for copy in group:
             copy.wait_send()
     hid_copy.wait()
+    for i in range(n):
+        for d in range(1, n):
+            red_copy(i, d).wait_send()
     for g in range(n):
         pltpu.make_async_remote_copy(
             src_ref=zin.at[0],
@@ -247,6 +265,8 @@
         in_specs=[hbm] * 5,
         out_specs=(hbm,) * 3,
         scratch_shapes=[
+            pltpu.VMEM((3, rows, inner), bf16),
+            pltpu.VMEM((depth, rows), bf16),
             pltpu.VMEM((3, n, rows, wide), bf16),
             pltpu.VMEM((n * cut, inner), bf16),
             pltpu.VMEM((n, heads * rows, n * rows), bf16),
@@ -256,7 +276,7 @@
             pltpu.VMEM((n, n - 1, cut, rows), bf16),
             pltpu.VMEM((n, cut, rows), bf16),
             pltpu.VMEM((n, cut, rows), bf16),
-            dma((5,)),
+            dma((6,)),
             dma((3, n - 1)),
             dma((3, n - 1)),
             dma((2,)),
@@ -281,26 +301,29 @@
         ),
         in_specs=[hbm] * 3,
         out_specs=(hbm,) * 2,
-        scratch_shapes=[pltpu.VMEM((depth, rows), bf16)] * 3 + [dma((4,))],
+        scratch_shapes=[pltpu.VMEM((depth, rows), bf16)] * 3 + [pltpu.VMEM((rows, inner), bf16), dma((5,))],
         compiler_params=pltpu.CompilerParams(vmem_limit_bytes=60 * 2**20),
     )(carried, branch, context)
     return (handed.T[None], context[None])
 
 
-def finish_kernel(carried, branch, context, handed, context_out, first, second, summed, sem):
+def finish_kernel(carried, branch, context, handed, context_out, first, second, summed, kept, sem):
     depth = handed.shape[0]
-    kept = pltpu.make_async_copy(context, context_out, sem.at[0])
-    one = pltpu.make_async_copy(carried, first, sem.at[1])
-    two = pltpu.make_async_copy(branch.at[pl.ds(0, depth)], second, sem.at[2])
-    for copy in (one, two, kept):
+    one = pltpu.make_async_copy(carried, first, sem.at[0])
+    two = pltpu.make_async_copy(branch.at[pl.ds(0, depth)], second, sem.at[1])
+    three = pltpu.make_async_copy(context, kept, sem.at[2])
+    for copy in (one, two, three):
         copy.start()
+    three.wait()
+    last = pltpu.make_async_copy(kept, context_out, sem.at[3])
+    last.start()
     one.wait()
     two.wait()
     summed[...] = (first[...].astype(jnp.float32) + second[...].astype(jnp.float32)).astype(jnp.bfloat16)
-    last = pltpu.make_async_copy(summed, handed, sem.at[3])
-    last.start()
+    result = pltpu.make_async_copy(summed, handed, sem.at[4])
+    result.start()
     last.wait()
-    kept.wait()
+    result.wait()
 
 
 def from_behind(block, axis, distance):

time: 50.4 us -> 46.4 us (0.921)
  Pallas kernels: 49.6 us -> 45.6 us
    pallas_call x1, Pallas kernels: 5.11 us -> 1.92 us  [relay_body(): pl.pallas_call(finish_kernel, out_shape=(jax.ShapeDtypeStruct((depth, row...]
    pallas_call x1, Pallas kernels: 44.5 us -> 43.7 us  [relay_body(): pl.pallas_call(functools.partial(relay_kernel, n, (2, 1, 3, 0)), out_shap...]
where the time goes in v5:
time: 46.4 us; the launch traced here: 46.3 us
  Pallas kernels  45.6 us (98%)
  between operations  0.64 us (1%)
    pallas_call x1, Pallas kernels, relay_body(): pl.pallas_call(functools.partial(relay_kernel, n, (2, 1, 3, 0)), out_shap...  43.7 us
    pallas_call x1, Pallas kernels, relay_body(): pl.pallas_call(finish_kernel, out_shape=(jax.ShapeDtypeStruct((depth, row...  1.92 us

profile of v5, /device:TPU:1, one launch (start us, length us, event | category | flops | bytes accessed | tf_op | source)
XLA Modules:
  0.0 46.3 jit_solution(10406584749112416249)
XLA Ops:
  0.6 43.7 %shard_map.68 = (bf16[1216,128]{1,0:T(8,128)(2,1)}, bf16[1168,128]{1,0:T(8,128)(2,1)}, bf16[128,512]{1,0:T(8,128)(2,1)}) custom-call(bf16[128,512]{1,0:T(8,128)(2,1)} %bitcast.13, bf16[128,512]{1,0:T(8,128)(2,1)} %bitcast.14, bf16[128,512]{1,0:T(8,128)(2,1)} %bitcast.15, bf16[1168,512]{1,0:T(8,128)(2,1)} %bitcast.11, bf16[1168,128]{1,0:T(8,128)(2,1)} %bitcast.12), custom_call_target="tpu_custom_call" | custom-call | tf_op jit(solution)/shard_map/pallas_call | solution.py:258
  44.4 1.9 %shard_map.69 = (bf16[1168,128]{1,0:T(8,128)(2,1)}, bf16[128,512]{1,0:T(8,128)(2,1)}) custom-call(bf16[1168,128]{1,0:T(8,128)(2,1)} %get-tuple-element.7.carried, bf16[1216,128]{1,0:T(8,128)(2,1)} %get-tuple-element.8.branch, bf16[128,512]{1,0:T(8,128)(2,1)} %get-tuple-element.9.context), custom_call_target="tpu_custom_call" | custom-call | tf_op jit(solution)/shard_map/pallas_call | solution.py:296

commit v6 on v5

--- a/solution.py
+++ b/solution.py
@@ -18,7 +18,6 @@
 
 def relay_kernel(
     n,
-    shifts,
     q_hbm,
     k_hbm,
     v_hbm,
@@ -138,15 +137,66 @@
             picked = jnp.where(lane == h, both[h * rows : (h + 1) * rows], picked)
         ctx[r, :, columns(c)] = (picked / total[r]).astype(jnp.bfloat16)
 
+    inner = (c == 1) | (c == 2)
+    mate = c + 1 - 2 * lax.rem(c, 2)
+    far = jnp.where(c < 2, 2, 0)
+    far_inner = jnp.where(c < 2, 2, 1)
+
+    def pair_block(plane, i):
+        return jnp.where(plane < 2, n - 1 - i, i)
+
+    def block_of(plane, i):
+        if i < 2:
+            return pair_block(plane, i)
+        return pair_block(plane, jnp.where((plane == 1) | (plane == 2), 5 - i, i))
+
+    def ctx_copy(block, kind, i, arrival, target):
+        return pltpu.make_async_remote_copy(
+            src_ref=block,
+            dst_ref=block,
+            send_sem=ctx_send.at[kind, i],
+            recv_sem=ctx_recv.at[arrival, i],
+            device_id=(s, target, m),
+            device_id_type=MESH,
+        )
+
+    def when(condition, action):
+        @pl.when(condition)
+        def _():
+            action()
+
+    def to_mate(i):
+        return ctx_copy(ctx.at[block_of(mate, i), :, columns(c)], 0, i, 0, mate)
+
+    def to_far(i):
+        block = ctx.at[pair_block(far_inner, i), :, columns(c)]
+        return ctx_copy(block, 1, i, 1 + lax.rem(c, 2), far_inner)
+
+    def relayed(i):
+        both = pl.ds(pl.multiple_of(far * wide, wide), 2 * wide)
+        return ctx_copy(ctx.at[pair_block(c, i), :, both], 2, i, 3, mate)
+
     def share(i):
-        group = []
-        for d in range(1, n):
-            j = lax.rem(c + d, n)
-            block = ctx.at[lax.rem(j + shifts[i], n), :, columns(c)]
-            group.append(send(block, block, ctx_send.at[i, d - 1], ctx_recv.at[i, d - 1], (s, j, m)))
-        ctx_copies.append(group)
-
-    ctx_copies = []
+        to_far(i).start()
+        to_mate(i).start()
+
+    def relay(i):
+        for k in range(2):
+            block = ctx.at[pair_block(c, i), :, columns(far + k)]
+            ctx_copy(block, 1, i, 1 + k, far_inner).wait_recv()
+        relayed(i).start()
+
+    def arrive(i):
+        for k in ((i,), (i,), (2, 3), ())[i]:
+            when(inner, lambda: relay(k))
+        when(~inner, lambda: relayed(i).wait_recv())
+        ctx_copy(ctx.at[block_of(c, i), :, columns(mate)], 0, i, 0, mate).wait_recv()
+
+    def ctx_sent(i):
+        to_far(i).wait_send()
+        to_mate(i).wait_send()
+        when(inner, lambda: relayed(i).wait_send())
+
     share(0)
     share(1)
     own[4].wait()
@@ -165,17 +215,8 @@
         )
 
     def project(i):
-        for d in range(1, n):
-            block = ctx.at[lax.rem(c + shifts[i], n), :, columns(lax.rem(c + d, n))]
-            pltpu.make_async_remote_copy(
-                src_ref=block,
-                dst_ref=block,
-                send_sem=ctx_send.at[i, d - 1],
-                recv_sem=ctx_recv.at[i, n - 1 - d],
-                device_id=(s, lax.rem(c + d, n), m),
-                device_id_type=MESH,
-            ).wait_recv()
-        r = lax.rem(c + shifts[i], n)
+        arrive(i)
+        r = block_of(c, i)
 
         @pl.loop(1, n + 1)
         def _(d):
@@ -187,7 +228,15 @@
             def _():
                 red_copy(i, d).start()
 
-    z_copies = []
+    def z_copy(i, source, target):
+        return pltpu.make_async_remote_copy(
+            src_ref=zsrc.at[i],
+            dst_ref=zin.at[source],
+            send_sem=z_send.at[i],
+            recv_sem=z_recv.at[source],
+            device_id=(s, target, m),
+            device_id_type=MESH,
+        )
 
     def reduce(i):
         for d in range(1, n):
@@ -195,21 +244,20 @@
         acc = part[i, m].astype(jnp.float32)
         for d in range(1, n):
             acc = acc + red[i, d - 1].astype(jnp.float32)
-        if shifts[i] == 0:
-            zin[i] = acc.astype(jnp.bfloat16)
+        if i == n - 1:
+            zin[c] = acc.astype(jnp.bfloat16)
         else:
             zsrc[i] = acc.astype(jnp.bfloat16)
-            target = lax.rem(c + shifts[i], n)
-            z_copies.append(send(zsrc.at[i], zin.at[i], z_send.at[i], z_recv.at[i], (s, target, m)))
+            z_copy(i, c, block_of(c, i)).start()
 
     out_copies = []
 
-    def hand_over(i):
-        if shifts[i]:
-            z_copies[i].wait_recv()
-        target = lax.rem(c + n - shifts[i], n)
+    def hand_over(source, own_plane=False):
+        if not own_plane:
+            z_copy(0, source, source).wait_recv()
+        slot = len(out_copies)
         piece = branch_out.at[pl.ds(pl.multiple_of(m * cut, cut), cut)]
-        out_copies.append(send(zin.at[i], piece, out_send.at[i], out_recv.at[m], (other, c, target)))
+        out_copies.append(send(zin.at[source], piece, out_send.at[slot], out_recv.at[m], (other, c, source)))
 
     project(0)
     for i in range(2, n):
@@ -220,19 +268,23 @@
     project(n - 1)
     ctx_back = pltpu.make_async_copy(ctx.at[c], ctx_out, local_sem.at[5])
     ctx_back.start()
-    for i in range(n - 3, n):
-        reduce(i)
-        if i < n - 1:
-            hand_over(i - 1)
-    hand_over(n - 1)
-    hand_over(n - 2)
+    reduce(1)
+    reduce(2)
+    hand_over(far)
+    hand_over(far + 1)
+    reduce(3)
+    hand_over(c, own_plane=True)
+    hand_over(mate)
 
     ctx_back.wait()
-    for group in qkv_copies + ctx_copies + [z_copies, out_copies]:
+    for group in qkv_copies + [out_copies]:
         for copy in group:
             copy.wait_send()
     hid_copy.wait()
     for i in range(n):
+        ctx_sent(i)
+        if i < n - 1:
+            z_copy(i, c, block_of(c, i)).wait_send()
         for d in range(1, n):
             red_copy(i, d).wait_send()
     for g in range(n):
@@ -256,7 +308,7 @@
     dma = pltpu.SemaphoreType.DMA
     hbm = pl.BlockSpec(memory_space=pltpu.HBM)
     branch, carried, context = pl.pallas_call(
-        functools.partial(relay_kernel, n, (2, 1, 3, 0)),
+        functools.partial(relay_kernel, n),
         out_shape=(
             jax.ShapeDtypeStruct((n * cut, rows), bf16),
             jax.ShapeDtypeStruct((depth, rows), bf16),
@@ -280,8 +332,8 @@
             dma((3, n - 1)),
             dma((3, n - 1)),
             dma((2,)),
-            dma((n, n - 1)),
-            dma((n, n - 1)),
+            dma((3, n)),
+            dma((4, n)),
             dma((n, n - 1)),
             dma((n, n - 1)),
             dma((n,)),

time: 46.4 us -> 46.5 us (level)
  no operation moved by 1% of the time
where the time goes in v6:
time: 46.5 us; the launch traced here: 46.1 us
  Pallas kernels  45.4 us (98%)
  between operations  0.64 us (1%)
    pallas_call x1, Pallas kernels, relay_body(): pl.pallas_call(functools.partial(relay_kernel, n), out_shape=(jax.ShapeDt...  43.5 us
    pallas_call x1, Pallas kernels, relay_body(): pl.pallas_call(finish_kernel, out_shape=(jax.ShapeDtypeStruct((depth, row...  1.92 us

profile of v6, /device:TPU:1, one launch (start us, length us, event | category | flops | bytes accessed | tf_op | source)
XLA Modules:
  0.0 46.1 jit_solution(326096540087154099)
XLA Ops:
  0.6 43.5 %shard_map.68 = (bf16[1216,128]{1,0:T(8,128)(2,1)}, bf16[1168,128]{1,0:T(8,128)(2,1)}, bf16[128,512]{1,0:T(8,128)(2,1)}) custom-call(bf16[128,512]{1,0:T(8,128)(2,1)} %bitcast.13, bf16[128,512]{1,0:T(8,128)(2,1)} %bitcast.14, bf16[128,512]{1,0:T(8,128)(2,1)} %bitcast.15, bf16[1168,512]{1,0:T(8,128)(2,1)} %bitcast.11, bf16[1168,128]{1,0:T(8,128)(2,1)} %bitcast.12), custom_call_target="tpu_custom_call" | custom-call | tf_op jit(solution)/shard_map/pallas_call | solution.py:310
  44.1 1.9 %shard_map.69 = (bf16[1168,128]{1,0:T(8,128)(2,1)}, bf16[128,512]{1,0:T(8,128)(2,1)}) custom-call(bf16[1168,128]{1,0:T(8,128)(2,1)} %get-tuple-element.7.carried, bf16[1216,128]{1,0:T(8,128)(2,1)} %get-tuple-element.8.branch, bf16[128,512]{1,0:T(8,128)(2,1)} %get-tuple-element.9.context), custom_call_target="tpu_custom_call" | custom-call | tf_op jit(solution)/shard_map/pallas_call | solution.py:348

commit v7 on v6

--- a/solution.py
+++ b/solution.py
@@ -30,9 +30,11 @@
     hid,
     qkv,
     w,
+    w_pair,
     expo,
     total,
     ctx,
+    ctx_pair,
     part,
     red,
     zsrc,
@@ -43,6 +45,8 @@
     hid_sem,
     ctx_send,
     ctx_recv,
+    pair_send,
+    pair_recv,
     red_send,
     red_recv,
     z_send,
@@ -54,6 +58,10 @@
     c = lax.axis_index("ctx")
     m = lax.axis_index("mp")
     other = 1 - s
+    x_mate = m + 1 - 2 * lax.rem(m, 2)
+    y_mate = lax.rem(m + 2, n)
+    pair_mate = jnp.where(s == 0, x_mate, y_mate)
+    sum_mate = jnp.where(s == 0, y_mate, x_mate)
     wide = ctx.shape[2] // n
     rows = ctx.shape[1]
     depth = w_hbm.shape[0]
@@ -102,6 +110,11 @@
                 send(staged.at[i, :, columns(j)], qkv.at[i, c], qkv_send.at[i, d - 1], qkv_recv.at[i, d - 1], (s, j, m))
             )
         qkv_copies.append(group)
+    own[3].wait()
+    w_copies = []
+    for i, t in enumerate((pair_mate, n - 1 - m)):
+        piece = w.at[pl.ds(pl.multiple_of(t * cut, cut), cut)]
+        w_copies.append(send(piece, w_pair.at[i], pair_send.at[3, i], pair_recv.at[3, i], (s, c, pair_mate)))
     for i in range(3):
         qkv[i, c] = staged[i, :, columns(c)]
 
@@ -176,9 +189,24 @@
         both = pl.ds(pl.multiple_of(far * wide, wide), 2 * wide)
         return ctx_copy(ctx.at[pair_block(c, i), :, both], 2, i, 3, mate)
 
+    def pass_on(kind, i):
+        first = (c, mate, far)[kind]
+        width = wide * (1, 1, 2)[kind]
+        span = pl.ds(pl.multiple_of(first * wide, wide), width)
+        r = block_of(c, i)
+        return pltpu.make_async_remote_copy(
+            src_ref=ctx.at[r, :, span],
+            dst_ref=ctx_pair.at[r, :, span],
+            send_sem=pair_send.at[kind, i],
+            recv_sem=pair_recv.at[kind, i],
+            device_id=(s, c, pair_mate),
+            device_id_type=MESH,
+        )
+
     def share(i):
         to_far(i).start()
         to_mate(i).start()
+        pass_on(0, i).start()
 
     def relay(i):
         for k in range(2):
@@ -190,7 +218,9 @@
         for k in ((i,), (i,), (2, 3), ())[i]:
             when(inner, lambda: relay(k))
         when(~inner, lambda: relayed(i).wait_recv())
+        pass_on(2, i).start()
         ctx_copy(ctx.at[block_of(c, i), :, columns(mate)], 0, i, 0, mate).wait_recv()
+        pass_on(1, i).start()
 
     def ctx_sent(i):
         to_far(i).wait_send()
@@ -201,32 +231,35 @@
     share(1)
     own[4].wait()
     hid_copy = send(hid, hid_out, hid_sem.at[0], hid_sem.at[1], (other, c, m))
-    own[3].wait()
-
-    def red_copy(i, d):
-        t = lax.rem(m + d, n)
+
+    def red_copy(i):
         return pltpu.make_async_remote_copy(
-            src_ref=part.at[i, t],
-            dst_ref=red.at[i, d - 1],
-            send_sem=red_send.at[i, d - 1],
-            recv_sem=red_recv.at[i, d - 1],
-            device_id=(s, c, t),
+            src_ref=part.at[i, 1],
+            dst_ref=red.at[i],
+            send_sem=red_send.at[i],
+            recv_sem=red_recv.at[i],
+            device_id=(s, c, sum_mate),
             device_id_type=MESH,
         )
 
     def project(i):
-        arrive(i)
+        for kind in range(3):
+            pass_on(kind, i).wait_recv()
+        if i == 0:
+            for copy in w_copies:
+                copy.wait_recv()
         r = block_of(c, i)
 
-        @pl.loop(1, n + 1)
-        def _(d):
-            t = lax.rem(m + d, n)
+        @pl.loop(0, 2)
+        def _(k):
+            t = jnp.where(k == 0, sum_mate, m)
             piece = w[pl.ds(pl.multiple_of(t * cut, cut), cut), :]
-            part[i, t] = dot(piece, ctx[r], NT).astype(jnp.bfloat16)
-
-            @pl.when(d < n)
+            both = dot(piece, ctx[r], NT) + dot(w_pair[1 - k], ctx_pair[r], NT)
+            part[i, 1 - k] = both.astype(jnp.bfloat16)
+
+            @pl.when(k == 0)
             def _():
-                red_copy(i, d).start()
+                red_copy(i).start()
 
     def z_copy(i, source, target):
         return pltpu.make_async_remote_copy(
@@ -239,11 +272,8 @@
         )
 
     def reduce(i):
-        for d in range(1, n):
-            red_copy(i, d).wait_recv()
-        acc = part[i, m].astype(jnp.float32)
-        for d in range(1, n):
-            acc = acc + red[i, d - 1].astype(jnp.float32)
+        red_copy(i).wait_recv()
+        acc = part[i, 0].astype(jnp.float32) + red[i].astype(jnp.float32)
         if i == n - 1:
             zin[c] = acc.astype(jnp.bfloat16)
         else:
@@ -259,16 +289,17 @@
         piece = branch_out.at[pl.ds(pl.multiple_of(m * cut, cut), cut)]
         out_copies.append(send(zin.at[source], piece, out_send.at[slot], out_recv.at[m], (other, c, source)))
 
-    project(0)
-    for i in range(2, n):
-        share(i)
-        project(i - 1)
-        if i > 2:
-            reduce(i - 3)
-    project(n - 1)
+    arrive(0)
+    for i in range(n - 1):
+        if i + 2 < n:
+            share(i + 2)
+        arrive(i + 1)
+        project(i)
+        if i > 0:
+            reduce(i - 1)
     ctx_back = pltpu.make_async_copy(ctx.at[c], ctx_out, local_sem.at[5])
     ctx_back.start()
-    reduce(1)
+    project(n - 1)
     reduce(2)
     hand_over(far)
     hand_over(far + 1)
@@ -277,7 +308,7 @@
     hand_over(mate)
 
     ctx_back.wait()
-    for group in qkv_copies + [out_copies]:
+    for group in qkv_copies + [w_copies, out_copies]:
         for copy in group:
             copy.wait_send()
     hid_copy.wait()
@@ -285,8 +316,9 @@
         ctx_sent(i)
         if i < n - 1:
             z_copy(i, c, block_of(c, i)).wait_send()
-        for d in range(1, n):
-            red_copy(i, d).wait_send()
+        red_copy(i).wait_send()
+        for kind in range(3):
+            pass_on(kind, i).wait_send()
     for g in range(n):
         pltpu.make_async_remote_copy(
             src_ref=zin.at[0],
@@ -321,11 +353,13 @@
             pltpu.VMEM((depth, rows), bf16),
             pltpu.VMEM((3, n, rows, wide), bf16),
             pltpu.VMEM((n * cut, inner), bf16),
+            pltpu.VMEM((2, cut, inner), bf16),
             pltpu.VMEM((n, heads * rows, n * rows), bf16),
             pltpu.VMEM((n, rows, wide), jnp.float32),
             pltpu.VMEM((n, rows, inner), bf16),
-            pltpu.VMEM((n, n, cut, rows), bf16),
-            pltpu.VMEM((n, n - 1, cut, rows), bf16),
+            pltpu.VMEM((n, rows, inner), bf16),
+            pltpu.VMEM((n, 2, cut, rows), bf16),
+            pltpu.VMEM((n, cut, rows), bf16),
             pltpu.VMEM((n, cut, rows), bf16),
             pltpu.VMEM((n, cut, rows), bf16),
             dma((6,)),
@@ -334,8 +368,10 @@
             dma((2,)),
             dma((3, n)),
             dma((4, n)),
-            dma((n, n - 1)),
-            dma((n, n - 1)),
+            dma((4, n)),
+            dma((4, n)),
+            dma((n,)),
+            dma((n,)),
             dma((n,)),
             dma((n,)),
             dma((n,)),

time: 46.5 us -> 52.7 us (1.13)
  Pallas kernels: 45.4 us -> 51.9 us
    pallas_call x1, Pallas kernels: 43.5 us -> 50 us  [relay_body(): pl.pallas_call(functools.partial(relay_kernel, n), out_shape=(jax.ShapeDt...]
where the time goes in v7:
time: 52.7 us; the launch traced here: 52.6 us
  Pallas kernels  51.9 us (98%)
  between operations  0.64 us (1%)
    pallas_call x1, Pallas kernels, relay_body(): pl.pallas_call(functools.partial(relay_kernel, n), out_shape=(jax.ShapeDt...  50 us
    pallas_call x1, Pallas kernels, relay_body(): pl.pallas_call(finish_kernel, out_shape=(jax.ShapeDtypeStruct((depth, row...  1.92 us

profile of v7, /device:TPU:1, one launch (start us, length us, event | category | flops | bytes accessed | tf_op | source)
XLA Modules:
  0.0 52.6 jit_solution(14892884539177205453)
XLA Ops:
  0.6 50.0 %shard_map.68 = (bf16[1216,128]{1,0:T(8,128)(2,1)}, bf16[1168,128]{1,0:T(8,128)(2,1)}, bf16[128,512]{1,0:T(8,128)(2,1)}) custom-call(bf16[128,512]{1,0:T(8,128)(2,1)} %bitcast.13, bf16[128,512]{1,0:T(8,128)(2,1)} %bitcast.14, bf16[128,512]{1,0:T(8,128)(2,1)} %bitcast.15, bf16[1168,512]{1,0:T(8,128)(2,1)} %bitcast.11, bf16[1168,128]{1,0:T(8,128)(2,1)} %bitcast.12), custom_call_target="tpu_custom_call" | custom-call | tf_op jit(solution)/shard_map/pallas_call | solution.py:342
  50.7 1.9 %shard_map.69 = (bf16[1168,128]{1,0:T(8,128)(2,1)}, bf16[128,512]{1,0:T(8,128)(2,1)}) custom-call(bf16[1168,128]{1,0:T(8,128)(2,1)} %get-tuple-element.7.carried, bf16[1216,128]{1,0:T(8,128)(2,1)} %get-tuple-element.8.branch, bf16[128,512]{1,0:T(8,128)(2,1)} %get-tuple-element.9.context), custom_call_target="tpu_custom_call" | custom-call | tf_op jit(solution)/shard_map/pallas_call | solution.py:384

commit v8 on v5

--- a/solution.py
+++ b/solution.py
@@ -55,6 +55,14 @@
     c = lax.axis_index("ctx")
     m = lax.axis_index("mp")
     other = 1 - s
+    x_mate = m + 1 - 2 * lax.rem(m, 2)
+    y_mate = lax.rem(m + 2, n)
+    first_mate = jnp.where(s == 0, x_mate, y_mate)
+    second_mate = jnp.where(s == 0, y_mate, x_mate)
+
+    def mate(d):
+        return jnp.where(d == 1, first_mate, jnp.where(d == 2, second_mate, jnp.where(d == 3, n - 1 - m, m)))
+
     wide = ctx.shape[2] // n
     rows = ctx.shape[1]
     depth = w_hbm.shape[0]
@@ -103,6 +111,8 @@
                 send(staged.at[i, :, columns(j)], qkv.at[i, c], qkv_send.at[i, d - 1], qkv_recv.at[i, d - 1], (s, j, m))
             )
         qkv_copies.append(group)
+    own[4].wait()
+    hid_copy = send(hid, hid_out, hid_sem.at[0], hid_sem.at[1], (other, c, m))
     for i in range(3):
         qkv[i, c] = staged[i, :, columns(c)]
 
@@ -149,12 +159,10 @@
     ctx_copies = []
     share(0)
     share(1)
-    own[4].wait()
-    hid_copy = send(hid, hid_out, hid_sem.at[0], hid_sem.at[1], (other, c, m))
     own[3].wait()
 
     def red_copy(i, d):
-        t = lax.rem(m + d, n)
+        t = mate(d)
         return pltpu.make_async_remote_copy(
             src_ref=part.at[i, t],
             dst_ref=red.at[i, d - 1],
@@ -179,7 +187,7 @@
 
         @pl.loop(1, n + 1)
         def _(d):
-            t = lax.rem(m + d, n)
+            t = mate(d)
             piece = w[pl.ds(pl.multiple_of(t * cut, cut), cut), :]
             part[i, t] = dot(piece, ctx[r], NT).astype(jnp.bfloat16)
 

time: 46.4 us -> 45.4 us (0.978)
  Pallas kernels: 45.6 us -> 44.3 us
    pallas_call x1, Pallas kernels: 43.7 us -> 42.4 us  [relay_body(): pl.pallas_call(functools.partial(relay_kernel, n, (2, 1, 3, 0)), out_shap...]
where the time goes in v8:
time: 45.4 us; the launch traced here: 44.9 us
  Pallas kernels  44.3 us (98%)
  between operations  0.64 us (1%)
    pallas_call x1, Pallas kernels, relay_body(): pl.pallas_call(functools.partial(relay_kernel, n, (2, 1, 3, 0)), out_shap...  42.4 us
    pallas_call x1, Pallas kernels, relay_body(): pl.pallas_call(finish_kernel, out_shape=(jax.ShapeDtypeStruct((depth, row...  1.92 us

profile of v8, /device:TPU:1, one launch (start us, length us, event | category | flops | bytes accessed | tf_op | source)
XLA Modules:
  0.0 44.9 jit_solution(6548730685454877521)
XLA Ops:
  0.6 42.4 %shard_map.68 = (bf16[1216,128]{1,0:T(8,128)(2,1)}, bf16[1168,128]{1,0:T(8,128)(2,1)}, bf16[128,512]{1,0:T(8,128)(2,1)}) custom-call(bf16[128,512]{1,0:T(8,128)(2,1)} %bitcast.13, bf16[128,512]{1,0:T(8,128)(2,1)} %bitcast.14, bf16[128,512]{1,0:T(8,128)(2,1)} %bitcast.15, bf16[1168,512]{1,0:T(8,128)(2,1)} %bitcast.11, bf16[1168,128]{1,0:T(8,128)(2,1)} %bitcast.12), custom_call_target="tpu_custom_call" | custom-call | tf_op jit(solution)/shard_map/pallas_call | solution.py:266
  43.0 1.9 %shard_map.69 = (bf16[1168,128]{1,0:T(8,128)(2,1)}, bf16[128,512]{1,0:T(8,128)(2,1)}) custom-call(bf16[1168,128]{1,0:T(8,128)(2,1)} %get-tuple-element.7.carried, bf16[1216,128]{1,0:T(8,128)(2,1)} %get-tuple-element.8.branch, bf16[128,512]{1,0:T(8,128)(2,1)} %get-tuple-element.9.context), custom_call_target="tpu_custom_call" | custom-call | tf_op jit(solution)/shard_map/pallas_call | solution.py:304

commit v9 on v8

--- a/solution.py
+++ b/solution.py
@@ -162,15 +162,21 @@
     own[3].wait()
 
     def red_copy(i, d):
-        t = mate(d)
+        target = mate(d) if i == n - 1 else jnp.where(d == 3, first_mate, mate(d))
         return pltpu.make_async_remote_copy(
-            src_ref=part.at[i, t],
+            src_ref=part.at[i, mate(d)],
             dst_ref=red.at[i, d - 1],
             send_sem=red_send.at[i, d - 1],
             recv_sem=red_recv.at[i, d - 1],
-            device_id=(s, c, t),
+            device_id=(s, c, target),
             device_id_type=MESH,
         )
+
+    def combine(i):
+        red_copy(i, 3).wait_recv()
+        both = part[i, second_mate].astype(jnp.float32) + red[i, 2].astype(jnp.float32)
+        part[i, second_mate] = both.astype(jnp.bfloat16)
+        red_copy(i, 2).start()
 
     def project(i):
         for d in range(1, n):
@@ -186,22 +192,22 @@
         r = lax.rem(c + shifts[i], n)
 
         @pl.loop(1, n + 1)
-        def _(d):
+        def _(step):
+            d = jnp.where(step == 2, 3, jnp.where(step == 3, 2, step))
             t = mate(d)
             piece = w[pl.ds(pl.multiple_of(t * cut, cut), cut), :]
             part[i, t] = dot(piece, ctx[r], NT).astype(jnp.bfloat16)
 
-            @pl.when(d < n)
+            @pl.when((d < n) if i == n - 1 else (step < 3))
             def _():
                 red_copy(i, d).start()
 
     z_copies = []
 
     def reduce(i):
-        for d in range(1, n):
+        acc = part[i, m].astype(jnp.float32)
+        for d in (1, 2, 3) if i == n - 1 else (1, 2):
             red_copy(i, d).wait_recv()
-        acc = part[i, m].astype(jnp.float32)
-        for d in range(1, n):
             acc = acc + red[i, d - 1].astype(jnp.float32)
         if shifts[i] == 0:
             zin[i] = acc.astype(jnp.bfloat16)
@@ -220,20 +226,24 @@
         out_copies.append(send(zin.at[i], piece, out_send.at[i], out_recv.at[m], (other, c, target)))
 
     project(0)
-    for i in range(2, n):
-        share(i)
-        project(i - 1)
-        if i > 2:
-            reduce(i - 3)
-    project(n - 1)
+    share(2)
+    project(1)
+    share(3)
+    combine(0)
+    project(2)
+    combine(1)
+    reduce(0)
+    project(3)
     ctx_back = pltpu.make_async_copy(ctx.at[c], ctx_out, local_sem.at[5])
     ctx_back.start()
-    for i in range(n - 3, n):
-        reduce(i)
-        if i < n - 1:
-            hand_over(i - 1)
-    hand_over(n - 1)
-    hand_over(n - 2)
+    combine(2)
+    reduce(1)
+    hand_over(0)
+    reduce(2)
+    hand_over(1)
+    reduce(3)
+    hand_over(3)
+    hand_over(2)
 
     ctx_back.wait()
     for group in qkv_copies + ctx_copies + [z_copies, out_copies]:

time: 45.4 us -> 48.4 us (1.066)
  the two profiles are of different devices: /device:TPU:1 before, /device:TPU:23 now
where the time goes in v9:
time: 48.4 us; the launch traced here: 48.2 us
  Pallas kernels  47.6 us (98%)
  between operations  0.64 us (1%)
    pallas_call x1, Pallas kernels, relay_body(): pl.pallas_call(functools.partial(relay_kernel, n, (2, 1, 3, 0)), out_shap...  45.7 us
    pallas_call x1, Pallas kernels, relay_body(): pl.pallas_call(finish_kernel, out_shape=(jax.ShapeDtypeStruct((depth, row...  1.92 us

profile of v9, /device:TPU:23, one launch (start us, length us, event | category | flops | bytes accessed | tf_op | source)
XLA Modules:
  0.0 48.2 jit_solution(10858614771927275379)
XLA Ops:
  0.6 45.7 %shard_map.68 = (bf16[1216,128]{1,0:T(8,128)(2,1)}, bf16[1168,128]{1,0:T(8,128)(2,1)}, bf16[128,512]{1,0:T(8,128)(2,1)}) custom-call(bf16[128,512]{1,0:T(8,128)(2,1)} %bitcast.13, bf16[128,512]{1,0:T(8,128)(2,1)} %bitcast.14, bf16[128,512]{1,0:T(8,128)(2,1)} %bitcast.15, bf16[1168,512]{1,0:T(8,128)(2,1)} %bitcast.11, bf16[1168,128]{1,0:T(8,128)(2,1)} %bitcast.12), custom_call_target="tpu_custom_call" | custom-call | tf_op jit(solution)/shard_map/pallas_call | solution.py:276
  46.3 1.9 %shard_map.69 = (bf16[1168,128]{1,0:T(8,128)(2,1)}, bf16[128,512]{1,0:T(8,128)(2,1)}) custom-call(bf16[1168,128]{1,0:T(8,128)(2,1)} %get-tuple-element.7.carried, bf16[1216,128]{1,0:T(8,128)(2,1)} %get-tuple-element.8.branch, bf16[128,512]{1,0:T(8,128)(2,1)} %get-tuple-element.9.context), custom_call_target="tpu_custom_call" | custom-call | tf_op jit(solution)/shard_map/pallas_call | solution.py:314

commit v10 on v8

--- a/solution.py
+++ b/solution.py
@@ -159,6 +159,7 @@
     ctx_copies = []
     share(0)
     share(1)
+    share(2)
     own[3].wait()
 
     def red_copy(i, d):
@@ -220,20 +221,20 @@
         out_copies.append(send(zin.at[i], piece, out_send.at[i], out_recv.at[m], (other, c, target)))
 
     project(0)
-    for i in range(2, n):
-        share(i)
-        project(i - 1)
-        if i > 2:
-            reduce(i - 3)
-    project(n - 1)
+    share(3)
+    project(1)
+    project(2)
+    reduce(0)
+    project(3)
+    reduce(1)
+    reduce(2)
     ctx_back = pltpu.make_async_copy(ctx.at[c], ctx_out, local_sem.at[5])
     ctx_back.start()
-    for i in range(n - 3, n):
-        reduce(i)
-        if i < n - 1:
-            hand_over(i - 1)
-    hand_over(n - 1)
-    hand_over(n - 2)
+    hand_over(0)
+    hand_over(1)
+    reduce(3)
+    hand_over(3)
+    hand_over(2)
 
     ctx_back.wait()
     for group in qkv_copies + ctx_copies + [z_copies, out_copies]:

time: 45.4 us -> 46.3 us (1.020)
  Pallas kernels: 44.3 us -> 45.5 us
    pallas_call x1, Pallas kernels: 42.4 us -> 43.6 us  [relay_body(): pl.pallas_call(functools.partial(relay_kernel, n, (2, 1, 3, 0)), out_shap...]
where the time goes in v10:
time: 46.3 us; the launch traced here: 46.1 us
  Pallas kernels  45.5 us (98%)
  between operations  0.64 us (1%)
    pallas_call x1, Pallas kernels, relay_body(): pl.pallas_call(functools.partial(relay_kernel, n, (2, 1, 3, 0)), out_shap...  43.6 us
    pallas_call x1, Pallas kernels, relay_body(): pl.pallas_call(finish_kernel, out_shape=(jax.ShapeDtypeStruct((depth, row...  1.92 us

profile of v10, /device:TPU:1, one launch (start us, length us, event | category | flops | bytes accessed | tf_op | source)
XLA Modules:
  0.0 46.1 jit_solution(17109038639461279953)
XLA Ops:
  0.6 43.6 %shard_map.68 = (bf16[1216,128]{1,0:T(8,128)(2,1)}, bf16[1168,128]{1,0:T(8,128)(2,1)}, bf16[128,512]{1,0:T(8,128)(2,1)}) custom-call(bf16[128,512]{1,0:T(8,128)(2,1)} %bitcast.13, bf16[128,512]{1,0:T(8,128)(2,1)} %bitcast.14, bf16[128,512]{1,0:T(8,128)(2,1)} %bitcast.15, bf16[1168,512]{1,0:T(8,128)(2,1)} %bitcast.11, bf16[1168,128]{1,0:T(8,128)(2,1)} %bitcast.12), custom_call_target="tpu_custom_call" | custom-call | tf_op jit(solution)/shard_map/pallas_call | solution.py:267
  44.2 1.9 %shard_map.69 = (bf16[1168,128]{1,0:T(8,128)(2,1)}, bf16[128,512]{1,0:T(8,128)(2,1)}) custom-call(bf16[1168,128]{1,0:T(8,128)(2,1)} %get-tuple-element.7.carried, bf16[1216,128]{1,0:T(8,128)(2,1)} %get-tuple-element.8.branch, bf16[128,512]{1,0:T(8,128)(2,1)} %get-tuple-element.9.context), custom_call_target="tpu_custom_call" | custom-call | tf_op jit(solution)/shard_map/pallas_call | solution.py:305

commit v11 on v8

--- a/solution.py
+++ b/solution.py
@@ -61,7 +61,7 @@
     second_mate = jnp.where(s == 0, y_mate, x_mate)
 
     def mate(d):
-        return jnp.where(d == 1, first_mate, jnp.where(d == 2, second_mate, jnp.where(d == 3, n - 1 - m, m)))
+        return jnp.where(d == 1, n - 1 - m, jnp.where(d == 2, first_mate, jnp.where(d == 3, second_mate, m)))
 
     wide = ctx.shape[2] // n
     rows = ctx.shape[1]

time: 45.4 us -> 45.8 us (level)
  Pallas kernels: 44.3 us -> 45 us
    pallas_call x1, Pallas kernels: 42.4 us -> 43 us  [relay_body(): pl.pallas_call(functools.partial(relay_kernel, n, (2, 1, 3, 0)), out_shap...]
where the time goes in v11:
time: 45.8 us; the launch traced here: 45.6 us
  Pallas kernels  45 us (98%)
  between operations  0.64 us (1%)
    pallas_call x1, Pallas kernels, relay_body(): pl.pallas_call(functools.partial(relay_kernel, n, (2, 1, 3, 0)), out_shap...  43 us
    pallas_call x1, Pallas kernels, relay_body(): pl.pallas_call(finish_kernel, out_shape=(jax.ShapeDtypeStruct((depth, row...  1.92 us

profile of v11, /device:TPU:1, one launch (start us, length us, event | category | flops | bytes accessed | tf_op | source)
XLA Modules:
  0.0 45.6 jit_solution(4162449652556413544)
XLA Ops:
  0.6 43.0 %shard_map.68 = (bf16[1216,128]{1,0:T(8,128)(2,1)}, bf16[1168,128]{1,0:T(8,128)(2,1)}, bf16[128,512]{1,0:T(8,128)(2,1)}) custom-call(bf16[128,512]{1,0:T(8,128)(2,1)} %bitcast.13, bf16[128,512]{1,0:T(8,128)(2,1)} %bitcast.14, bf16[128,512]{1,0:T(8,128)(2,1)} %bitcast.15, bf16[1168,512]{1,0:T(8,128)(2,1)} %bitcast.11, bf16[1168,128]{1,0:T(8,128)(2,1)} %bitcast.12), custom_call_target="tpu_custom_call" | custom-call | tf_op jit(solution)/shard_map/pallas_call | solution.py:266
  43.7 1.9 %shard_map.69 = (bf16[1168,128]{1,0:T(8,128)(2,1)}, bf16[128,512]{1,0:T(8,128)(2,1)}) custom-call(bf16[1168,128]{1,0:T(8,128)(2,1)} %get-tuple-element.7.carried, bf16[1216,128]{1,0:T(8,128)(2,1)} %get-tuple-element.8.branch, bf16[128,512]{1,0:T(8,128)(2,1)} %get-tuple-element.9.context), custom_call_target="tpu_custom_call" | custom-call | tf_op jit(solution)/shard_map/pallas_call | solution.py:304
